TPU v7x, 256 devices: a whole 4x4x8 slice. The times are simulated.
256 devices in a mesh: dp: 8 (over z), mp: 16 (over y, x), section: 2 (over core).
Axes of the slice: x: 4, y: 4, z: 8, core: 2. Of those that a mesh axis runs over, the one named last changes fastest.
Arguments:
- acts: bfloat16 [2, 4096, 6144], P('section', 'dp', 'mp'), may hold values from -6 to 6
- halting: int32 [2, 4096], P('section', 'dp'), may hold values from 0 to 2, as said below
- norm_gain: float32 [2, 6144], P('section'), may hold values from 0.1 to 1.9
- qkv_weight: bfloat16 [2, 6144, 12288], P('section', None, 'mp'), may hold values from -0.078125 to 0.078125
- qk_gain: float32 [2, 2, 32, 128], P('section', None, 'mp'), may hold values from 0.5 to 11, as said below
- out_weight: bfloat16 [2, 4096, 6144], P('section', None, 'mp'), may hold values from -0.09375 to 0.09375
Outputs:
- mixed: bfloat16 [2, 4096, 6144], P('section', 'dp', 'mp')
Inputs may be any that keep to these rules, and one draw needn't show every extreme that they name: `halting`: A token of segment s takes part in that segment's layer exactly when its value is greater than s. Among the 512 tokens of one device at one segment at most 384 are live, exactly 384 on some device of every segment, and at least 128. `qk_gain`: Positive.
All inputs are finite; a program needn't handle non-finite values.
Results may differ from a plain program's by a relative error of at most 0.012.
Values may be sent and summed in bfloat16 or wider, within the bound.
A program may use at most 128 MiB of HBM per device.

v0:
```python
import math

import jax
import jax.numpy as jnp
from jax import lax
from jax.sharding import PartitionSpec as P

HEAD = 128
GROUP = 4


def partner(block, axis, distance):
    count = lax.axis_size(axis)
    route = []
    for low in range(count):
        high = low | 1 << distance
        if high != low and high < count:
            route += [(low, high), (high, low)]
    return lax.ppermute(block, axis, route)


def passed_along(x, axis, by):
    length = lax.axis_size(axis)
    return lax.ppermute(x, axis, [(i, (i + by) % length) for i in range(length)])


def row_norm(values, gain):
    mean = jnp.mean(values, axis=-1, keepdims=True)
    centred = values - mean
    spread = jnp.mean(centred * centred, axis=-1, keepdims=True)
    return centred * lax.rsqrt(spread + 1e-06) * gain


def body(acts, halting, norm_gain, qkv_weight, qk_gain, out_weight):
    segment = lax.axis_index("section")
    tokens = acts[0]
    live = halting[0] > segment
    whole = lax.all_gather(tokens, "mp", axis=1, tiled=True)
    normed = row_norm(whole.astype(jnp.float32), norm_gain[0]).astype(jnp.bfloat16)
    count = tokens.shape[0]
    heads_here = qk_gain.shape[2]
    qkv = jnp.dot(normed, qkv_weight[0], preferred_element_type=jnp.float32).reshape(
        count, heads_here, 3, HEAD
    )
    query = row_norm(qkv[:, :, 0], qk_gain[0, 0]).astype(jnp.bfloat16)
    keys = row_norm(qkv[:, :, 1], qk_gain[0, 1]).astype(jnp.bfloat16)
    values = qkv[:, :, 2].astype(jnp.bfloat16)
    flags = live.astype(jnp.bfloat16)
    for bit in range(GROUP.bit_length() - 1):
        other_keys, other_values, other_flags = partner((keys, values, flags), "dp", bit)
        keys = jnp.concatenate([keys, other_keys], axis=0)
        values = jnp.concatenate([values, other_values], axis=0)
        flags = jnp.concatenate([flags, other_flags], axis=0)
    scores = jnp.einsum(
        "qhe,khe->hqk", query, keys, preferred_element_type=jnp.float32
    ) / math.sqrt(HEAD)
    scores = jnp.where(flags[None, None, :] > 0.5, scores, -jnp.inf)
    top = jnp.max(scores, axis=-1, keepdims=True)
    weights = jnp.exp(scores - top)
    total = jnp.sum(weights, axis=-1)
    rounded = weights.astype(jnp.bfloat16)
    summed = jnp.einsum("hqk,khe->qhe", rounded, values, preferred_element_type=jnp.float32)
    heads_out = (
        (summed / jnp.transpose(total)[:, :, None])
        .astype(jnp.bfloat16)
        .reshape(count, heads_here * HEAD)
    )
    projection = out_weight[0]
    projected = jnp.dot(
        lax.all_gather(heads_out, "mp", axis=1, tiled=True),
        projection,
        preferred_element_type=jnp.float32,
    )
    wide = tokens.astype(jnp.float32)
    result = jnp.where(live[:, None], wide + projected, wide).astype(jnp.bfloat16)
    passed = passed_along(result, "section", 1)
    return passed[None]


def solution(mesh):
    return jax.shard_map(
        body,
        mesh=mesh,
        in_specs=(
            P("section", "dp", "mp"),
            P("section", "dp"),
            P("section", None),
            P("section", None, "mp"),
            P("section", None, "mp", None),
            P("section", None, "mp"),
        ),
        out_specs=P("section", "dp", "mp"),
        check_vma=False,
    )
```

profile of v0, /device:TPU:1, one launch (start us, length us, event | category | flops | bytes accessed | tf_op | source)
XLA Modules:
  0.0 233.1 jit_solution(17968423120511250464)
XLA Ops:
  6.5 0.0 copy-start
  6.5 0.0 all-gather.6.cloned.1.call-start
  6.5 0.7 all-gather.6.cloned.1.call-update
  7.3 0.0 copy-start.5
  7.3 0.0 all-gather.4.cloned.1.call-start
  7.3 0.0 copy-start.6
  7.3 12.8 %copy.9 = bf16[1,6144,768]{1,2,0:T(8,128)(2,1)} copy(bf16[1,6144,768]{2,1,0:T(8,128)(2,1)} %param.9) | data formatting | bytes 18874368 | tf_op args[3]
  20.2 0.0 copy-done.5
  20.2 65.4 %all-gather.6.cloned.1.call-done = bf16[1,512,6144]{2,1,0:T(8,128)(2,1)} async-done(((bf16[1,512,384]{2,1,0:T(8,128)(2,1)}), bf16[1,512,6144]{2,1,0:T(8,128)(2,1)}) %all-gather.6.cloned.1.call-update) | async-done | bytes 6291472 | tf_op jit(solution)/shard_map/all_gather | solution.py:38
  85.5 0.0 copy-start.1
  85.5 3.8 %convert_reduce_fusion = f32[512]{0:T(512)S(1)} fusion(bf16[1,512,6144]{2,1,0:T(8,128)(2,1)} %all-gather.6.cloned.1.call-done), kind=kLoop, calls=%fused_computation | loop fusion | flops 6290944 | bytes 6293504 | tf_op jit(solution)/shard_map/reduce_sum | solution.py:28
  89.4 0.7 copy-done.1
  90.1 1.8 fusion.3
  91.9 0.0 copy-done.6
  91.9 0.0 copy-start.4
  91.9 9.9 %fusion.10 = f32[512,2,3,128]{3,0,2,1:T(8,128)S(1)} fusion(bf16[2,3,128,6144]{3,2,1,0:T(8,128)(2,1)} %bitcast.72, bf16[1,512,6144]{2,1,0:T(8,128)(2,1)S(1)} %copy-done.1, f32[6144]{0:T(1024)S(1)} %bitcast.76, f32[512]{0:T(512)S(1)} %add_rsqrt_fusion.2, f32[512]{0:T(512)S(1)} %broadcast_multiply_fusion.2), kind=kOutput, calls=%fused_computation.14 | convolution fusion | flops 4847566848 | bytes 17330176 | tf_op jit(solution)/shard_map/dot_general | solution.py:42
  101.8 0.0 copy-start.2
  101.8 0.4 slice_reduce_fusion.1
  102.2 0.6 multiply_reduce_fusion.1
  102.9 0.1 copy-done.2
  103.0 0.3 multiply_convert_fusion
  103.3 1.4 collective-permute-start.4
  104.7 0.0 copy-done.4
  104.7 0.3 collective-permute-start.2
  105.0 4.8 %collective-permute-done.2 = bf16[512]{0:T(512)(128)(2,1)S(1)} collective-permute-done((bf16[512]{0:T(512)(128)(2,1)S(1)}, bf16[512]{0:T(512)(128)(2,1)S(1)}, u32[]{:S(2)}, u32[]{:S(2)}) %collective-permute-start.2) | collective-permute-done | bytes 1056 | tf_op jit(solution)/shard_map/ppermute | solution.py:19
  109.8 2.3 collective-permute-start.3
  112.0 0.0 collective-permute-done.4
  112.0 1.0 pad_maximum_fusion.1
  113.0 0.2 collective-permute-start.5
  113.2 1.1 fusion.53
  114.3 1.4 collective-permute-start
  115.7 0.0 collective-permute-done.3
  115.7 11.7 %collective-permute-done = bf16[512,2,128]{2,0,1:T(8,128)(2,1)S(1)} collective-permute-done((bf16[512,2,128]{2,0,1:T(8,128)(2,1)S(1)}, bf16[512,2,128]{2,0,1:T(8,128)(2,1)S(1)}, u32[]{:S(2)}, u32[]{:S(2)}) %collective-permute-start) | collective-permute-done | bytes 262176 | tf_op jit(solution)/shard_map/ppermute | solution.py:19
  127.5 4.1 %collective-permute-start.1 = (bf16[1024,2,128]{2,0,1:T(8,128)(2,1)S(1)}, bf16[1024,2,128]{2,0,1:T(8,128)(2,1)S(1)}, u32[]{:S(2)}, u32[]{:S(2)}) collective-permute-start(bf16[1024,2,128]{2,0,1:T(8,128)(2,1)S(1)} %pad_maximum_fusion), channel_id=1, source_target_pairs={{0,64},{64,0},{32,96},{96,32},{128,192},{192,128},{160,224},{224,1... | collective-permute-start | bytes 1572872 | tf_op jit(solution)/shard_map/ppermute | solution.py:19
  131.6 17.8 %collective-permute-done.5 = bf16[1024,2,128]{2,0,1:T(8,128)(2,1)S(1)} collective-permute-done((bf16[1024,2,128]{2,0,1:T(8,128)(2,1)S(1)}, bf16[1024,2,128]{2,0,1:T(8,128)(2,1)S(1)}, u32[]{:S(2)}, u32[]{:S(2)}) %collective-permute-start.5) | collective-permute-done | bytes 524320 | tf_op jit(solution)/shard_map/ppermute | solution.py:19
  149.4 2.6 %fusion.6 = (f32[2,512]{1,0:T(2,128)S(1)}, f32[2,512,2048]{2,1,0:T(8,128)S(1)}) fusion(pred[2048]{0:T(1024)(128)(4,1)S(1)} %maximum_compare_fusion, bf16[1024,2,128]{2,0,1:T(8,128)(2,1)S(1)} %collective-permute-done.5, bf16[512,2,128]{2,0,1:T(8,128)(2,1)} %collective-permute-done.4, bf16[512,2,128]{2,0,1:T(8,128)(2,1)S(1)} %multiply_convert_fusion, ...), kind=kOutput, calls=%fused_computation.10 | convolution fusion | flops 546831360 | bytes 9976832 | tf_op jit(solution)/shard_map/qhe,khe->hqk/dot_general | solution.py:54
  152.0 1.9 fusion.7
  153.9 0.0 copy-start.3
  153.9 6.8 %collective-permute-done.1 = bf16[1024,2,128]{2,0,1:T(8,128)(2,1)S(1)} collective-permute-done((bf16[1024,2,128]{2,0,1:T(8,128)(2,1)S(1)}, bf16[1024,2,128]{2,0,1:T(8,128)(2,1)S(1)}, u32[]{:S(2)}, u32[]{:S(2)}) %collective-permute-start.1) | collective-permute-done | bytes 524320 | tf_op jit(solution)/shard_map/ppermute | solution.py:19
  160.7 3.0 %fusion.48 = bf16[512,2,128]{0,2,1:T(8,128)(2,1)} fusion(f32[2,512,2048]{2,1,0:T(8,128)S(1)} %get-tuple-element.12, f32[2,512]{1,0:T(2,128)S(1)} %get-tuple-element.11, pred[2048]{0:T(1024)(128)(4,1)S(1)} %maximum_compare_fusion, bf16[1024,2,128]{2,0,1:T(8,128)(2,1)S(1)} %collective-permute-done.1, bf16[512,2,128]{2,0,1:T(8,128)(2,1)S(1)} %collective-permute-done, ...), kind=kOutput, calls=%fused_computation.38 | convolution fusion | flops 548667392 | bytes 9709568 | tf_op jit(solution)/shard_map/hqk,khe->qhe/dot_general | solution.py:62
  163.6 0.0 all-gather.4.cloned.1.call-update
  163.6 55.1 %all-gather.4.cloned.1.call-done = bf16[512,4096]{0,1:T(8,128)(2,1)} async-done(((bf16[512,256]{0,1:T(8,128)(2,1)}), bf16[512,4096]{0,1:T(8,128)(2,1)}) %all-gather.4.cloned.1.call-update) | async-done | bytes 4194320 | tf_op jit(solution)/shard_map/all_gather | solution.py:70
  218.8 0.0 copy-done
  218.8 0.0 copy-done.3
  218.8 4.6 %fusion.26 = bf16[512,384]{1,0:T(8,128)(2,1)S(1)} fusion(bf16[512,4096]{0,1:T(8,128)(2,1)} %all-gather.4.cloned.1.call-done, bf16[1,4096,384]{2,1,0:T(8,128)(2,1)S(1)} %copy-done, bf16[1,512,384]{2,1,0:T(8,128)(2,1)S(1)} %copy-done.3, pred[512]{0:T(512)(128)(4,1)S(1)} %compare_reduce_fusion), kind=kOutput, calls=%fused_computation.24 | convolution fusion | flops 1611399168 | bytes 8126976 | tf_op jit(solution)/shard_map/dot_general | solution.py:69
  223.4 0.8 collective-permute-start.6
  224.1 1.3 collective-permute-done.6
  225.5 0.7 copy.14
  (11 shorter events, 0.1 us)
Async XLA Ops:
  6.5 212.2 %copy-start = (bf16[1,4096,384]{2,1,0:T(8,128)(2,1)S(1)}, bf16[1,4096,384]{2,1,0:T(8,128)(2,1)}, u32[]{:S(2)}) copy-start(bf16[1,4096,384]{2,1,0:T(8,128)(2,1)} %param.11) | copy-start | bytes 9437188
  6.5 79.0 %all-gather.6.cloned.1.call-start = ((), (), s32[]{:S(2)}) async-start(), calls=%async_computation.1 | async-start | bytes 6684672 | tf_op jit(solution)/shard_map/all_gather | solution.py:38
  7.3 12.9 %copy-start.5 = (f32[1,2,2,128]{3,2,1,0:T(2,128)S(1)}, f32[1,2,2,128]{3,2,1,0:T(2,128)}, u32[]{:S(2)}) copy-start(f32[1,2,2,128]{3,2,1,0:T(2,128)} %param.10) | copy-start | bytes 6148
  7.3 211.5 %all-gather.4.cloned.1.call-start = ((), (), s32[]{:S(2)}) async-start(), calls=%async_computation | async-start | bytes 4456448 | tf_op jit(solution)/shard_map/all_gather | solution.py:70
  7.3 84.6 %copy-start.6 = (f32[1,6144]{1,0:T(1,128)S(1)}, f32[1,6144]{1,0:T(1,128)}, u32[]{:S(2)}) copy-start(f32[1,6144]{1,0:T(1,128)} %param.8) | copy-start | bytes 73732
  85.5 4.6 %copy-start.1 = (bf16[1,512,6144]{2,1,0:T(8,128)(2,1)S(1)}, bf16[1,512,6144]{2,1,0:T(8,128)(2,1)}, u32[]{:S(2)}) copy-start(bf16[1,512,6144]{2,1,0:T(8,128)(2,1)} %all-gather.6.cloned.1.call-done) | copy-start | bytes 18874372
  91.9 12.7 %copy-start.4 = (s32[1,512]{1,0:T(1,128)S(1)}, s32[1,512]{1,0:T(1,128)}, u32[]{:S(2)}) copy-start(s32[1,512]{1,0:T(1,128)} %param.7) | copy-start | bytes 6148
  101.8 1.2 copy-start.2
  103.3 8.7 %collective-permute-start.4 = (bf16[512,2,128]{2,0,1:T(8,128)(2,1)S(1)}, bf16[512,2,128]{2,0,1:T(8,128)(2,1)}, u32[]{:S(2)}, u32[]{:S(2)}) collective-permute-start(bf16[512,2,128]{2,0,1:T(8,128)(2,1)S(1)} %multiply_convert_fusion), channel_id=1, source_target_pairs={{0,32},{32,0},{64,96},{96,64},{128,160},{160,128},{192,224},{224,1... | collective-permute-start | bytes 786440 | tf_op jit(solution)/shard_map/ppermute | solution.py:19
  104.7 5.1 %collective-permute-start.2 = (bf16[512]{0:T(512)(128)(2,1)S(1)}, bf16[512]{0:T(512)(128)(2,1)S(1)}, u32[]{:S(2)}, u32[]{:S(2)}) collective-permute-start(bf16[512]{0:T(512)(128)(2,1)S(1)} %convert_element_type.37), channel_id=1, source_target_pairs={{0,32},{32,0},{64,96},{96,64},{128,160},{160,128},{192,224},{224,1... | collective-permute-start | bytes 3080 | tf_op jit(solution)/shard_map/ppermute | solution.py:19
  109.8 5.9 %collective-permute-start.3 = (bf16[1024]{0:T(1024)(128)(2,1)S(1)}, bf16[1024]{0:T(1024)(128)(2,1)S(1)}, u32[]{:S(2)}, u32[]{:S(2)}) collective-permute-start(bf16[1024]{0:T(1024)(128)(2,1)S(1)} %pad_maximum_fusion.2), channel_id=1, source_target_pairs={{0,64},{64,0},{32,96},{96,32},{128,192},{192,128},{160,224},{224,1... | collective-permute-start | bytes 6152 | tf_op jit(solution)/shard_map/ppermute | solution.py:19
  113.0 36.4 %collective-permute-start.5 = (bf16[1024,2,128]{2,0,1:T(8,128)(2,1)S(1)}, bf16[1024,2,128]{2,0,1:T(8,128)(2,1)S(1)}, u32[]{:S(2)}, u32[]{:S(2)}) collective-permute-start(bf16[1024,2,128]{2,0,1:T(8,128)(2,1)S(1)} %pad_maximum_fusion.1), channel_id=1, source_target_pairs={{0,64},{64,0},{32,96},{96,32},{128,192},{192,128},{160,224},{224,1... | collective-permute-start | bytes 1572872 | tf_op jit(solution)/shard_map/ppermute | solution.py:19
  114.3 13.1 %collective-permute-start = (bf16[512,2,128]{2,0,1:T(8,128)(2,1)S(1)}, bf16[512,2,128]{2,0,1:T(8,128)(2,1)S(1)}, u32[]{:S(2)}, u32[]{:S(2)}) collective-permute-start(bf16[512,2,128]{2,0,1:T(8,128)(2,1)S(1)} %fusion.53), channel_id=1, source_target_pairs={{0,32},{32,0},{64,96},{96,64},{128,160},{160,128},{192,224},{224,1... | collective-permute-start | bytes 786440 | tf_op jit(solution)/shard_map/ppermute | solution.py:19
  127.5 33.2 %collective-permute-start.1 = (bf16[1024,2,128]{2,0,1:T(8,128)(2,1)S(1)}, bf16[1024,2,128]{2,0,1:T(8,128)(2,1)S(1)}, u32[]{:S(2)}, u32[]{:S(2)}) collective-permute-start(bf16[1024,2,128]{2,0,1:T(8,128)(2,1)S(1)} %pad_maximum_fusion), channel_id=1, source_target_pairs={{0,64},{64,0},{32,96},{96,32},{128,192},{192,128},{160,224},{224,1... | collective-permute-start | bytes 1572872 | tf_op jit(solution)/shard_map/ppermute | solution.py:19
  153.9 64.9 %copy-start.3 = (bf16[1,512,384]{2,1,0:T(8,128)(2,1)S(1)}, bf16[1,512,384]{2,1,0:T(8,128)(2,1)}, u32[]{:S(2)}) copy-start(bf16[1,512,384]{2,1,0:T(8,128)(2,1)} %param.6) | copy-start | bytes 1179652
  223.4 2.1 collective-permute-start.6
Sparse Core Ops, SparseCore 0:
  9.8 75.7 all-gather.5
  163.8 54.9 all-gather.3
where the time goes:
time: 234 us; the launch traced here: 233 us
  waiting for transfers between devices  164 us (70%)
  matrix products  19.9 us (9%)
  local copies, waits for them, and re-layouts  15.6 us (7%)
  between operations  13.5 us (6%)
  starting transfers between devices  10.4 us (4%)
  other arithmetic  9.94 us (4%)
    all_gather x1, waiting for transfers between devices, body(): whole = lax.all_gather(tokens, 'mp', axis=1, tiled=True)  65.4 us
    all_gather x1, waiting for transfers between devices, body(): lax.all_gather(heads_out, 'mp', axis=1, tiled=True)  55.1 us
    ppermute x6, waiting for transfers between devices, partner(): return lax.ppermute(block, axis, route)  41.1 us
    unnamed x16, local copies, waits for them, and re-layouts  14.5 us
    dot_general x1, matrix products, body(): jnp.dot(normed, qkv_weight[0], preferred_element_type=jnp.float32)  9.86 us
    ppermute x6, starting transfers between devices, partner(): return lax.ppermute(block, axis, route)  9.58 us
  transfers between devices with their start and end apart: 9, of which 7 were waited for; matrix products, arithmetic and copies ran while one was open for 8% of the time, Pallas kernels for 0%

commit v1 on v0

v1 whole, which is shorter than its diff:
```python
import functools
import math

import jax
import jax.numpy as jnp
from jax import lax
from jax.experimental import pallas as pl
from jax.experimental.pallas import tpu as pltpu
from jax.sharding import PartitionSpec as P

MESH = pl.DeviceIdType.MESH
HEAD = 128
GROUP = 4
SIDE = 4
TOK = 512
LIVE = 384
FEAT = 384
HEADS_HERE = 2
WIDE = HEADS_HERE * HEAD
COLS = 3 * WIDE
ROWS = 128
CHUNKS = LIVE // ROWS
HALF = ROWS // 2
QUARTER = HALF // 2
SCALE = math.log2(math.e) / math.sqrt(HEAD)
F32 = jnp.float32
BF16 = jnp.bfloat16


class Gather:
    def __init__(self, buf, width, send, recv, x, y):
        self.buf, self.width, self.send, self.recv = buf, width, send, recv
        self.at = (y, x)
        self.started = []

    def ring(self, axis, by):
        return lax.rem(self.at[axis] + by + SIDE, SIDE)

    def device(self, axis, by):
        y, x = self.at
        if axis == 0:
            y = self.ring(0, by)
        else:
            x = self.ring(1, by)
        return {"mp": y * SIDE + x}

    def block(self, c, first, a, b, row, rows):
        y, x = (b, a) if first == 1 else (a, b)
        lanes = pl.ds(pl.multiple_of(x * self.width, 128), self.width)
        return self.buf.at[c, y, pl.ds(row, rows), lanes]

    def slab(self, c, first, b, row, low, count):
        if first == 1:
            return self.buf.at[c, b, pl.ds(row, HALF), pl.ds(low * self.width, count * self.width)]
        lanes = pl.ds(pl.multiple_of(b * self.width, 128), self.width)
        return self.buf.at[c, pl.ds(low, count), pl.ds(row, HALF), lanes]

    def copy(self, ref, c, first, k, device):
        at = (c * 2 + first) * 8 + k
        return pltpu.make_async_remote_copy(
            src_ref=ref,
            dst_ref=ref,
            send_sem=self.send.at[at],
            recv_sem=self.recv.at[at],
            device_id=device,
            device_id_type=MESH,
        )

    def step(self, c, stage):
        for first in (1, 0):
            self.half_step(c, stage, first)

    def half_step(self, c, stage, first):
        second = 1 - first
        row = 0 if first == 1 else HALF
        a, b = self.at[first], self.at[second]
        up, down = self.device(first, 1), self.device(first, -1)
        out, back = self.device(second, 1), self.device(second, -1)
        if stage >= 1:
            got = {
                1: lambda: (
                    self.block(c, first, self.ring(first, -1), b, row, HALF),
                    self.block(c, first, self.ring(first, 1), b, row, HALF),
                ),
                2: lambda: (
                    self.block(c, first, self.ring(first, 2), b, row, QUARTER),
                    self.block(c, first, self.ring(first, 2), b, row + QUARTER, QUARTER),
                ),
                3: lambda: (
                    self.slab(c, first, self.ring(second, -1), row, 0, SIDE),
                    self.slab(c, first, self.ring(second, 1), row, 0, SIDE),
                ),
                4: lambda: (
                    self.slab(c, first, self.ring(second, 2), row, 0, 2),
                    self.slab(c, first, self.ring(second, 2), row, 2, 2),
                ),
            }[stage]()
            for side in (0, 1):
                self.copy(got[side], c, first, (stage - 1) * 2 + side, up).wait_recv()
        if stage == 0:
            own = self.block(c, first, a, b, row, HALF)
            sends = ((own, up), (own, down))
        elif stage == 1:
            sends = (
                (self.block(c, first, self.ring(first, -1), b, row, QUARTER), up),
                (self.block(c, first, self.ring(first, 1), b, row + QUARTER, QUARTER), down),
            )
        elif stage == 2:
            own = self.slab(c, first, b, row, 0, SIDE)
            sends = ((own, out), (own, back))
        elif stage == 3:
            sends = (
                (self.slab(c, first, self.ring(second, -1), row, 0, 2), out),
                (self.slab(c, first, self.ring(second, 1), row, 2, 2), back),
            )
        else:
            sends = ()
        for side, (ref, device) in enumerate(sends):
            copy = self.copy(ref, c, first, stage * 2 + side, device)
            copy.start()
            self.started.append(copy)

    def finish(self):
        for copy in self.started:
            copy.wait_send()


class Line:
    def __init__(self, kv, send, recv, z):
        self.kv, self.send, self.recv, self.z = kv, send, recv, z
        self.p = lax.rem(z, GROUP)

    def copy(self, c, j, way):
        at = (c * 3 + j) * 2 + (0 if way > 0 else 1)
        ref = self.kv.at[self.p - way * j, c]
        return pltpu.make_async_remote_copy(
            src_ref=ref,
            dst_ref=ref,
            send_sem=self.send.at[at],
            recv_sem=self.recv.at[at],
            device_id={"dp": self.z + way},
            device_id_type=MESH,
        )

    def arriving(self, c, j, way):
        at = (c * 3 + j) * 2 + (0 if way > 0 else 1)
        ref = self.kv.at[self.p - way * (j + 1), c]
        return pltpu.make_async_remote_copy(
            src_ref=ref,
            dst_ref=ref,
            send_sem=self.send.at[at],
            recv_sem=self.recv.at[at],
            device_id={"dp": self.z - way},
            device_id_type=MESH,
        )

    def has(self, way, j):
        return self.p >= j if way > 0 else self.p + j < GROUP

    def sends(self, way, j):
        more = self.p < GROUP - 1 if way > 0 else self.p > 0
        return jnp.logical_and(more, self.has(way, j))

    def step(self, c, j):
        for way in (1, -1):
            if j > 0:
                pl.when(self.has(way, j))(lambda: self.arriving(c, j - 1, way).wait_recv())
            if j < 3:
                pl.when(self.sends(way, j))(lambda: self.copy(c, j, way).start())

    def finish(self):
        for c in range(CHUNKS):
            for j in range(3):
                for way in (1, -1):
                    pl.when(self.sends(way, j))(lambda: self.copy(c, j, way).wait_send())


def normed(values, gain):
    mean = jnp.mean(values, axis=-1, keepdims=True)
    centred = values - mean
    spread = jnp.mean(centred * centred, axis=-1, keepdims=True)
    return centred * lax.rsqrt(spread + 1e-06) * gain


def kernel(
    x_ref, halt_ref, gain_ref, qk_ref, w_hbm, wo_hbm, out_ref,
    w, wo, xg, xn, acc, kv, query, counts, flags, hg, pick, place, rest, result, outgoing,
    w_sem, a_send, a_recv, c_send, c_recv, z_send, z_recv, n_send, n_recv, o_send, o_recv,
):
    z = lax.axis_index("dp")
    m = lax.axis_index("mp")
    s = lax.axis_index("section")
    x, y = lax.rem(m, SIDE), m // SIDE
    p = lax.rem(z, GROUP)
    base = z - p

    barrier = pltpu.get_barrier_semaphore()
    peers = [{"dp": base + lax.rem(p + j, GROUP)} for j in (1, 2, 3)]
    neighbours = [
        {"mp": y * SIDE + lax.rem(x + 1, SIDE)},
        {"mp": y * SIDE + lax.rem(x + SIDE - 1, SIDE)},
        {"mp": lax.rem(y + 1, SIDE) * SIDE + x},
        {"mp": lax.rem(y + SIDE - 1, SIDE) * SIDE + x},
        {"section": 1 - s},
    ]
    for device in neighbours + peers:
        pl.semaphore_signal(barrier, inc=1, device_id=device, device_id_type=MESH)

    load_w = pltpu.make_async_copy(w_hbm, w, w_sem.at[0])
    load_wo = pltpu.make_async_copy(wo_hbm, wo, w_sem.at[1])
    load_w.start()
    load_wo.start()

    live = jnp.where(halt_ref[...] > s, 1.0, 0.0)
    before = lax.broadcasted_iota(jnp.int32, (TOK, TOK), 0) < lax.broadcasted_iota(jnp.int32, (TOK, TOK), 1)
    rank = jnp.dot(
        jnp.broadcast_to(live, (16, TOK)).astype(BF16),
        jnp.where(before, 1.0, 0.0).astype(BF16),
        preferred_element_type=F32,
    )[0:1]
    count = jnp.sum(live, axis=-1, keepdims=True)
    rank = jnp.where(live > 0.5, rank, -1.0)
    row = lax.broadcasted_iota(jnp.int32, (LIVE, TOK), 0).astype(F32)
    chosen = jnp.broadcast_to(rank, (LIVE, TOK)) == jnp.minimum(row, jnp.broadcast_to(count, (LIVE, TOK)) - 1.0)
    first = jnp.where(chosen, 1.0, 0.0)
    pick[...] = jnp.where(row < jnp.broadcast_to(count, (LIVE, TOK)), first, 0.0)
    compact = jnp.dot(first.astype(BF16), x_ref[...], preferred_element_type=F32).astype(BF16)
    own = pl.ds(pl.multiple_of(x * FEAT, 128), FEAT)
    for c in range(CHUNKS):
        xg[c, y, :, own] = compact[c * ROWS : (c + 1) * ROWS]
    counts[p] = jnp.broadcast_to(count, (8, 128))

    pl.semaphore_wait(barrier, 8)

    ga = Gather(xg, FEAT, a_send, a_recv, x, y)
    gc = Gather(hg, WIDE, c_send, c_recv, x, y)
    line = Line(kv, z_send, z_recv, z)

    def count_copy(j, ref, device):
        return pltpu.make_async_remote_copy(
            src_ref=ref,
            dst_ref=ref,
            send_sem=n_send.at[j],
            recv_sem=n_recv.at[j],
            device_id=device,
            device_id_type=MESH,
        )

    def project(c):
        def rows(i, _):
            at = pl.ds(pl.multiple_of(i * 16, 16), 16)
            total = jnp.zeros((16, 1), F32)
            for b in range(SIDE):
                total += jnp.sum(xg[c, b, at, :].astype(F32), axis=-1, keepdims=True)
            mean = total * (1.0 / (16 * FEAT))
            square = jnp.zeros((16, 1), F32)
            for b in range(SIDE):
                centred = xg[c, b, at, :].astype(F32) - mean
                square += jnp.sum(centred * centred, axis=-1, keepdims=True)
            scale = lax.rsqrt(square * (1.0 / (16 * FEAT)) + 1e-06)
            for b in range(SIDE):
                lanes = slice(b * SIDE * FEAT, (b + 1) * SIDE * FEAT)
                centred = xg[c, b, at, :].astype(F32) - mean
                xn[b, at, :] = (centred * scale * gain_ref[:, lanes]).astype(BF16)
            return 0

        lax.fori_loop(0, ROWS // 16, rows, 0)
        if c == 0:
            load_w.wait()
        acc[...] = jnp.zeros_like(acc)

        def part(b, _):
            depth = pl.ds(pl.multiple_of(b * SIDE * FEAT, 128), SIDE * FEAT)
            acc[...] += jnp.dot(xn[b], w[depth, :], preferred_element_type=F32)
            return 0

        lax.fori_loop(0, SIDE, part, 0)
        real = lax.broadcasted_iota(jnp.int32, (ROWS, HEAD), 0).astype(F32) + c * ROWS < jnp.broadcast_to(count, (ROWS, HEAD))
        for h in range(HEADS_HERE):
            col = h * 3 * HEAD
            query[c, h] = normed(acc[:, col : col + HEAD], qk_ref[0, h : h + 1, :]).astype(BF16)
            kv[p, c, :, h * HEAD : (h + 1) * HEAD] = normed(
                acc[:, col + HEAD : col + 2 * HEAD], qk_ref[1, h : h + 1, :]
            ).astype(BF16)
            kv[p, c, :, WIDE + h * HEAD : WIDE + (h + 1) * HEAD] = jnp.where(
                real, acc[:, col + 2 * HEAD : col + 3 * HEAD], 0.0
            ).astype(BF16)

    def attend(c):
        for h in range(HEADS_HERE):
            keys = kv[:, :, :, h * HEAD : (h + 1) * HEAD].reshape(GROUP * LIVE, HEAD)
            values = kv[:, :, :, WIDE + h * HEAD : WIDE + (h + 1) * HEAD].reshape(GROUP * LIVE, HEAD)
            scores = (
                lax.dot_general(query[c, h], keys, (((1,), (1,)), ((), ())), preferred_element_type=F32) * SCALE
            )
            top = jnp.max(scores, axis=-1, keepdims=True)
            weights = jnp.exp2(scores - top).astype(BF16)
            summed = jnp.dot(
                weights, jnp.concatenate([values, flags[...]], axis=1), preferred_element_type=F32
            )
            lanes = pl.ds(pl.multiple_of(x * WIDE + h * HEAD, 128), HEAD)
            hg[c, y, :, lanes] = (summed[:, :HEAD] / summed[:, HEAD:]).astype(BF16)

    def close(c):
        if c == 0:
            load_wo.wait()
        total = jnp.zeros((ROWS, FEAT), F32)
        for b in range(SIDE):
            total += jnp.dot(
                hg[c, b], wo[b * SIDE * WIDE : (b + 1) * SIDE * WIDE, :], preferred_element_type=F32
            )
        mine = xg[c, y, :, own].astype(F32)
        result[c * ROWS : (c + 1) * ROWS, :] = (mine + total).astype(BF16)
        low, high = c * ROWS, (c + 1) * ROWS if c < CHUNKS - 1 else TOK
        known = (c + 1) * ROWS
        placed = jnp.dot(place[low:high, :known], result[:known, :], preferred_element_type=F32)
        outgoing[low:high, :] = (rest[low:high, :].astype(F32) + placed).astype(BF16)
        copy = pltpu.make_async_remote_copy(
            src_ref=outgoing.at[pl.ds(low, high - low)],
            dst_ref=out_ref.at[pl.ds(low, high - low)],
            send_sem=o_send.at[c],
            recv_sem=o_recv.at[c],
            device_id={"section": 1 - s},
            device_id_type=MESH,
        )
        copy.start()
        return copy

    ga.step(0, 0)
    for j in (1, 2, 3):
        count_copy(j - 1, counts.at[p], peers[j - 1]).start()
    ga.step(1, 0)
    ga.step(0, 1)
    ga.step(0, 2)
    ga.step(1, 1)
    ga.step(2, 0)

    place[...] = jnp.transpose(pick[...]).astype(BF16)
    rest[...] = (
        x_ref[...].astype(F32) - jnp.dot(place[...], compact, preferred_element_type=F32)
    ).astype(BF16)
    for j in (1, 2, 3):
        count_copy(j - 1, counts.at[lax.rem(p + GROUP - j, GROUP)], peers[j - 1]).wait_recv()
    place_of = lax.broadcasted_iota(jnp.int32, (LIVE, HEAD), 0).astype(F32)
    for q in range(GROUP):
        flags[q * LIVE : (q + 1) * LIVE, :] = jnp.where(
            place_of < jnp.broadcast_to(counts[q, 0:1, :], (LIVE, HEAD)), 1.0, 0.0
        ).astype(BF16)

    ga.step(0, 3)
    ga.step(1, 2)
    ga.step(2, 1)
    ga.step(0, 4)
    project(0)
    line.step(0, 0)
    ga.step(1, 3)
    ga.step(2, 2)
    line.step(0, 1)
    ga.step(1, 4)
    line.step(0, 2)
    project(1)
    line.step(1, 0)
    ga.step(2, 3)
    line.step(0, 3)
    line.step(1, 1)
    ga.step(2, 4)
    project(2)
    line.step(2, 0)
    line.step(1, 2)
    line.step(2, 1)
    line.step(1, 3)
    line.step(2, 2)
    line.step(2, 3)

    attend(0)
    gc.step(0, 0)
    attend(1)
    gc.step(1, 0)
    gc.step(0, 1)
    attend(2)
    gc.step(0, 2)
    gc.step(1, 1)
    gc.step(2, 0)
    gc.step(0, 3)
    gc.step(1, 2)
    gc.step(2, 1)
    gc.step(0, 4)
    copies = [close(0)]
    gc.step(1, 3)
    gc.step(2, 2)
    gc.step(1, 4)
    copies.append(close(1))
    gc.step(2, 3)
    gc.step(2, 4)
    copies.append(close(2))

    for j in (1, 2, 3):
        count_copy(j - 1, counts.at[p], peers[j - 1]).wait_send()
    ga.finish()
    gc.finish()
    line.finish()
    for copy in copies:
        copy.wait()


def body(acts, halting, norm_gain, qkv_weight, qk_gain, out_weight):
    vmem = pl.BlockSpec(memory_space=pltpu.VMEM)
    anywhere = pl.BlockSpec(memory_space=pl.ANY)
    out = pl.pallas_call(
        kernel,
        out_shape=jax.ShapeDtypeStruct((TOK, FEAT), BF16),
        in_specs=[vmem, vmem, vmem, vmem, anywhere, anywhere],
        out_specs=anywhere,
        scratch_shapes=[
            pltpu.VMEM((16 * FEAT, COLS), BF16),
            pltpu.VMEM((16 * WIDE, FEAT), BF16),
            pltpu.VMEM((CHUNKS, SIDE, ROWS, SIDE * FEAT), BF16),
            pltpu.VMEM((SIDE, ROWS, SIDE * FEAT), BF16),
            pltpu.VMEM((ROWS, COLS), F32),
            pltpu.VMEM((GROUP, CHUNKS, ROWS, 2 * WIDE), BF16),
            pltpu.VMEM((CHUNKS, HEADS_HERE, ROWS, HEAD), BF16),
            pltpu.VMEM((GROUP, 8, 128), F32),
            pltpu.VMEM((GROUP * LIVE, HEAD), BF16),
            pltpu.VMEM((CHUNKS, SIDE, ROWS, SIDE * WIDE), BF16),
            pltpu.VMEM((LIVE, TOK), F32),
            pltpu.VMEM((TOK, LIVE), BF16),
            pltpu.VMEM((TOK, FEAT), BF16),
            pltpu.VMEM((LIVE, FEAT), BF16),
            pltpu.VMEM((TOK, FEAT), BF16),
            pltpu.SemaphoreType.DMA((2,)),
            pltpu.SemaphoreType.DMA((CHUNKS * 16,)),
            pltpu.SemaphoreType.DMA((CHUNKS * 16,)),
            pltpu.SemaphoreType.DMA((CHUNKS * 16,)),
            pltpu.SemaphoreType.DMA((CHUNKS * 16,)),
            pltpu.SemaphoreType.DMA((CHUNKS * 6,)),
            pltpu.SemaphoreType.DMA((CHUNKS * 6,)),
            pltpu.SemaphoreType.DMA((3,)),
            pltpu.SemaphoreType.DMA((3,)),
            pltpu.SemaphoreType.DMA((CHUNKS,)),
            pltpu.SemaphoreType.DMA((CHUNKS,)),
        ],
        compiler_params=pltpu.CompilerParams(
            collective_id=0, has_side_effects=True, vmem_limit_bytes=56 * 1024 * 1024
        ),
    )(acts[0], halting, norm_gain, qk_gain[0], qkv_weight[0], out_weight[0])
    return out[None]


def solution(mesh):
    return jax.shard_map(
        body,
        mesh=mesh,
        in_specs=(
            P("section", "dp", "mp"),
            P("section", "dp"),
            P("section", None),
            P("section", None, "mp"),
            P("section", None, "mp", None),
            P("section", None, "mp"),
        ),
        out_specs=P("section", "dp", "mp"),
        check_vma=False,
    )
```

time: 234 us -> 98.7 us (0.42)
  waiting for transfers between devices: 164 us -> 0 us
  Pallas kernels: 0 us -> 96.8 us
  matrix products: 19.9 us -> 0 us
  local copies, waits for them, and re-layouts: 15.6 us -> 1.78 us
  between operations: 13.5 us -> 0.01 us
  starting transfers between devices: 10.4 us -> 0 us
  other arithmetic: 9.94 us -> 0 us
    all_gather x2 -> x0, waiting for transfers between devices: 120 us -> none  [the longest x1 65.4 us: body(): whole = lax.all_gather(tokens, 'mp', axis=1, tiled=True)]
    pallas_call x0 -> x1, Pallas kernels: none -> 96.8 us  [body(): pl.pallas_call(kernel, out_shape=jax.ShapeDtypeStruct((TOK, FEAT), BF16),...]
    ppermute x7 -> x0, waiting for transfers between devices: 42.5 us -> none  [the longest x6 41.1 us: partner(): return lax.ppermute(block, axis, route)]
    dot_general x4 -> x0, matrix products: 19.9 us -> none  [the longest x1 9.86 us: body(): jnp.dot(normed, qkv_weight[0], preferred_element_type=jnp.float32)]
    unnamed x16 -> x1, local copies, waits for them, and re-layouts: 14.5 us -> 1.78 us
    ppermute x7 -> x0, starting transfers between devices: 10.3 us -> none  [the longest x6 9.58 us: partner(): return lax.ppermute(block, axis, route)]
    reduce_sum x5 -> x0, other arithmetic: 8.5 us -> none  [the longest x2 4.19 us: row_norm(): mean = jnp.mean(values, axis=-1, keepdims=True)]
  transfers between devices with their start and end apart: 9 -> 0, of which waited for: 7 -> 0; matrix products, arithmetic and copies ran while one was open for 8% -> 0% of each run, Pallas kernels for 0% -> 0%
where the time goes in v1:
time: 98.7 us; the launch traced here: 98.6 us
  Pallas kernels  96.8 us (98%)
  local copies, waits for them, and re-layouts  1.78 us (2%)
    pallas_call x1, Pallas kernels, body(): pl.pallas_call(kernel, out_shape=jax.ShapeDtypeStruct((TOK, FEAT), BF16),...  96.8 us

profile of v1, /device:TPU:1, one launch (start us, length us, event | category | flops | bytes accessed | tf_op | source)
XLA Modules:
  0.0 98.6 jit_solution(12306517355184200523)
XLA Ops:
  0.0 96.8 %shard_map.64 = bf16[512,384]{1,0:T(8,128)(2,1)} custom-call(bf16[512,384]{1,0:T(8,128)(2,1)} %bitcast.8, s32[1,512]{1,0:T(1,128)} %halt_ref.1, f32[1,6144]{1,0:T(1,128)} %gain_ref.1, f32[2,2,128]{2,1,0:T(2,128)} %bitcast.9, bf16[6144,768]{1,0:T(8,128)(2,1)} %bitcast.5, bf16[4096,384]{1,0:T(8,128)(2,1)} %bitcast.6), custom_call_target="tpu_custom_call" | custom-call | tf_op jit(solution)/shard_map/pallas_call | solution.py:409
  96.8 1.8 %copy.8 = bf16[1,512,384]{2,1,0:T(8,128)(2,1)} copy(bf16[1,512,384]{2,1,0:T(8,128)(2,1)} %bitcast.7) | data formatting | bytes 786432

commit v2 on v1

v2 whole, which is shorter than its diff:
```python
import functools
import math

import jax
import jax.numpy as jnp
from jax import lax
from jax.experimental import pallas as pl
from jax.experimental.pallas import tpu as pltpu
from jax.sharding import PartitionSpec as P

MESH = pl.DeviceIdType.MESH
HEAD = 128
GROUP = 4
SIDE = 4
TOK = 512
LIVE = 384
FEAT = 384
HEADS_HERE = 2
WIDE = HEADS_HERE * HEAD
COLS = 3 * WIDE
ROWS = 128
CHUNKS = LIVE // ROWS
SCALE = math.log2(math.e) / math.sqrt(HEAD)
F32 = jnp.float32
BF16 = jnp.bfloat16


PIECES_A = (
    (0, 32, 1, 0), (32, 32, 0, 0), (64, 64, 1, 0), (128, 64, 0, 0), (192, 64, 1, 0), (256, 64, 0, 0),
    (320, 32, 1, 0), (352, 32, 0, 0),
)
PIECES_C = ((0, 64, 1, 1), (64, 64, 0, 1), (128, 64, 1, 1), (192, 64, 0, 1), (256, 64, 1, 1), (320, 64, 0, 1))
PARTS = ((0, 64), (64, 128), (192, 128), (320, 64))

ORDER = (
    ("gate",), ("a", 0, 0), ("a", 1, 0), ("a", 2, 0), ("a", 3, 0), ("greet",), ("a", 0, 1), ("a", 1, 1), ("a", 4, 0), ("a", 5, 0),
    ("a", 2, 1), ("a", 3, 1), ("a", 6, 0), ("a", 7, 0), ("a", 4, 1), ("a", 5, 1), ("prepare",), ("a", 0, 2), ("a", 1, 2),
    ("project", 0), ("z", 0, 0), ("a", 6, 1), ("a", 7, 1), ("open",), ("a", 2, 2), ("a", 3, 2), ("project", 1), ("z", 1, 0),
    ("z", 0, 1), ("a", 4, 2), ("a", 5, 2), ("project", 2), ("z", 2, 0), ("z", 0, 2), ("z", 1, 1), ("a", 6, 2), ("a", 7, 2),
    ("project", 3), ("z", 3, 0), ("z", 0, 3), ("z", 1, 2), ("z", 2, 1), ("z", 1, 3), ("z", 3, 1), ("z", 2, 2), ("z", 2, 3), ("z", 3, 2), ("z", 3, 3),
    ("attend", 0), ("c", 0, 0), ("c", 1, 0), ("attend", 1), ("c", 2, 0), ("c", 3, 0), ("attend", 2), ("c", 4, 0), ("c", 5, 0),
    ("c", 0, 1), ("c", 1, 1), ("c", 2, 1), ("c", 3, 1), ("c", 4, 1), ("c", 5, 1),
    ("c", 0, 2), ("c", 1, 2), ("c", 2, 2), ("c", 3, 2), ("c", 4, 2), ("c", 5, 2), ("c", 0, 3), ("c", 1, 3), ("close", 0),
    ("c", 2, 3), ("c", 3, 3), ("close", 1), ("c", 4, 3), ("c", 5, 3), ("close", 2),
)


class Gather:
    def __init__(self, buf, pieces, send, recv, x, y):
        self.buf, self.pieces, self.send, self.recv = buf, pieces, send, recv
        self.at = (y, x)
        self.started = []

    def ring(self, axis, by):
        return lax.rem(self.at[axis] + by + SIDE, SIDE)

    def device(self, axis, by):
        y, x = self.at
        if axis == 0:
            y = self.ring(0, by)
        else:
            x = self.ring(1, by)
        return {"mp": y * SIDE + x}

    def copy(self, ref, n, k, device):
        at = n * 8 + k
        return pltpu.make_async_remote_copy(
            src_ref=ref,
            dst_ref=ref,
            send_sem=self.send.at[at],
            recv_sem=self.recv.at[at],
            device_id=device,
            device_id_type=MESH,
        )

    def plan(self, n):
        row, rows, first, way = self.pieces[n]
        second = 1 - first
        half = rows // 2

        def block(by, low=0, count=rows):
            a = self.ring(first, by)
            y, x = (self.at[0], a) if first == 1 else (a, self.at[1])
            return lambda: self.buf.at[y, x, pl.ds(row + low, count), :]

        def slab(by, low=0, count=SIDE):
            b = self.ring(second, by)
            if first == 1:
                return lambda: self.buf.at[b, pl.ds(low, count), pl.ds(row, rows), :]
            return lambda: self.buf.at[pl.ds(low, count), b, pl.ds(row, rows), :]

        whole = (1, -1, 2)
        if way < 2:
            sends = [[(k, block(0), first, d) for k, d in enumerate(whole)]]
            arrivals = [[(k, block(-d)) for k, d in enumerate(whole)]]
        else:
            sends = [
                [(0, block(0), first, 1), (1, block(0), first, -1)],
                [(2, block(-1, 0, half), first, 1), (3, block(1, half, half), first, -1)],
            ]
            arrivals = [[(0, block(-1)), (1, block(1))], [(2, block(2, 0, half)), (3, block(2, half, half))]]
        if way < 1:
            sends += [[(4 + k, slab(0), second, d) for k, d in enumerate(whole)]]
            arrivals += [[(4 + k, slab(-d)) for k, d in enumerate(whole)]]
        else:
            sends += [
                [(4, slab(0), second, 1), (5, slab(0), second, -1)],
                [(6, slab(-1, 0, 2), second, 1), (7, slab(1, 2, 2), second, -1)],
            ]
            arrivals += [[(4, slab(-1)), (5, slab(1))], [(6, slab(2, 0, 2)), (7, slab(2, 2, 2))]]
        return sends, arrivals

    def step(self, n, stage):
        sends, arrivals = self.plan(n)
        if stage > 0:
            for k, ref in arrivals[stage - 1]:
                self.copy(ref(), n, k, self.device(0, 1)).wait_recv()
        if stage < len(sends):
            for k, ref, axis, by in sends[stage]:
                copy = self.copy(ref(), n, k, self.device(axis, by))
                copy.start()
                self.started.append(copy)

    def finish(self):
        for copy in self.started:
            copy.wait_send()


class Line:
    def __init__(self, kv, send, recv, z):
        self.kv, self.send, self.recv, self.z = kv, send, recv, z
        self.p = lax.rem(z, GROUP)
        self.started = []

    def copy(self, c, j, way):
        at = (c * 3 + j) * 2 + (0 if way > 0 else 1)
        ref = self.kv.at[self.p - way * j, pl.ds(*PARTS[c])]
        return pltpu.make_async_remote_copy(
            src_ref=ref,
            dst_ref=ref,
            send_sem=self.send.at[at],
            recv_sem=self.recv.at[at],
            device_id={"dp": self.z + way},
            device_id_type=MESH,
        )

    def arriving(self, c, j, way):
        at = (c * 3 + j) * 2 + (0 if way > 0 else 1)
        ref = self.kv.at[self.p - way * (j + 1), pl.ds(*PARTS[c])]
        return pltpu.make_async_remote_copy(
            src_ref=ref,
            dst_ref=ref,
            send_sem=self.send.at[at],
            recv_sem=self.recv.at[at],
            device_id={"dp": self.z - way},
            device_id_type=MESH,
        )

    def has(self, way, j):
        return self.p >= j if way > 0 else self.p + j < GROUP

    def sends(self, way, j):
        more = self.p < GROUP - 1 if way > 0 else self.p > 0
        return jnp.logical_and(more, self.has(way, j))

    def step(self, c, j):
        if j < 3:
            self.started.append((c, j))
        for way in (1, -1):
            if j > 0:
                pl.when(self.has(way, j))(lambda: self.arriving(c, j - 1, way).wait_recv())
            if j < 3:
                pl.when(self.sends(way, j))(lambda: self.copy(c, j, way).start())

    def finish(self):
        for c, j in self.started:
            for way in (1, -1):
                pl.when(self.sends(way, j))(lambda: self.copy(c, j, way).wait_send())


def normed(values, gain):
    mean = jnp.mean(values, axis=-1, keepdims=True)
    centred = values - mean
    spread = jnp.mean(centred * centred, axis=-1, keepdims=True)
    return centred * lax.rsqrt(spread + 1e-06) * gain


def kernel(
    x_ref, halt_ref, gain_ref, qk_ref, w_hbm, wo_hbm, out_ref,
    w, wo, xg, xn, acc, kv, query, counts, flags, hg, pick, place, rest, result, outgoing,
    w_sem, a_send, a_recv, c_send, c_recv, z_send, z_recv, n_send, n_recv, o_send, o_recv, turn,
):
    z = lax.axis_index("dp")
    m = lax.axis_index("mp")
    s = lax.axis_index("section")
    x, y = lax.rem(m, SIDE), m // SIDE
    p = lax.rem(z, GROUP)
    base = z - p

    barrier = pltpu.get_barrier_semaphore()
    peers = [{"dp": base + lax.rem(p + j, GROUP)} for j in (1, 2, 3)]
    neighbours = [
        {"mp": y * SIDE + lax.rem(x + 1, SIDE)},
        {"mp": y * SIDE + lax.rem(x + SIDE - 1, SIDE)},
        {"mp": y * SIDE + lax.rem(x + 2, SIDE)},
        {"mp": lax.rem(y + 1, SIDE) * SIDE + x},
        {"mp": lax.rem(y + 2, SIDE) * SIDE + x},
        {"mp": lax.rem(y + SIDE - 1, SIDE) * SIDE + x},
        {"section": 1 - s},
    ]
    for device in neighbours + peers:
        pl.semaphore_signal(barrier, inc=1, device_id=device, device_id_type=MESH)

    load_w = pltpu.make_async_copy(w_hbm, w, w_sem.at[0])
    load_wo = pltpu.make_async_copy(wo_hbm, wo, w_sem.at[1])
    load_w.start()
    load_wo.start()

    live = jnp.where(halt_ref[...] > s, 1.0, 0.0)
    before = lax.broadcasted_iota(jnp.int32, (TOK, TOK), 0) < lax.broadcasted_iota(jnp.int32, (TOK, TOK), 1)
    rank = jnp.dot(
        jnp.broadcast_to(live, (16, TOK)).astype(BF16),
        jnp.where(before, 1.0, 0.0).astype(BF16),
        preferred_element_type=F32,
    )[0:1]
    count = jnp.sum(live, axis=-1, keepdims=True)
    rank = jnp.where(live > 0.5, rank, -1.0)
    row = lax.broadcasted_iota(jnp.int32, (LIVE, TOK), 0).astype(F32)
    chosen = jnp.broadcast_to(rank, (LIVE, TOK)) == jnp.minimum(row, jnp.broadcast_to(count, (LIVE, TOK)) - 1.0)
    first = jnp.where(chosen, 1.0, 0.0)
    pick[...] = jnp.where(row < jnp.broadcast_to(count, (LIVE, TOK)), first, 0.0)
    compact = jnp.dot(first.astype(BF16), x_ref[...], preferred_element_type=F32).astype(BF16)
    xg[y, x] = compact
    counts[p] = jnp.broadcast_to(count, (8, 128))

    pl.semaphore_wait(barrier, 10)

    ga = Gather(xg, PIECES_A, a_send, a_recv, x, y)
    gc = Gather(hg, PIECES_C, c_send, c_recv, x, y)
    line = Line(kv, z_send, z_recv, z)

    def count_copy(j, ref, device):
        return pltpu.make_async_remote_copy(
            src_ref=ref,
            dst_ref=ref,
            send_sem=n_send.at[j],
            recv_sem=n_recv.at[j],
            device_id=device,
            device_id_type=MESH,
        )

    def project(c):
        low, rows = PARTS[c]
        for at in range(low, low + rows, 64):
            at = slice(at, at + 64)
            total = jnp.zeros((64, 1), F32)
            for b in range(16):
                total += jnp.sum(xg[b // SIDE, b % SIDE, at].astype(F32), axis=-1, keepdims=True)
            mean = total * (1.0 / (16 * FEAT))
            square = jnp.zeros((64, 1), F32)
            for b in range(16):
                centred = xg[b // SIDE, b % SIDE, at].astype(F32) - mean
                square += jnp.sum(centred * centred, axis=-1, keepdims=True)
            scale = lax.rsqrt(square * (1.0 / (16 * FEAT)) + 1e-06)
            for b in range(16):
                lanes = slice(b * FEAT, (b + 1) * FEAT)
                centred = xg[b // SIDE, b % SIDE, at].astype(F32) - mean
                xn[at.start - low : at.stop - low, lanes] = (centred * scale * gain_ref[:, lanes]).astype(BF16)
        if c == 0:
            load_w.wait()
        total = jnp.zeros((rows, COLS), F32)
        for b in range(8):
            depth = slice(b * 2 * FEAT, (b + 1) * 2 * FEAT)
            total += jnp.dot(xn[:rows, depth], w[depth, :], preferred_element_type=F32)
        acc[:rows] = total
        at = slice(low, low + rows)
        real = lax.broadcasted_iota(jnp.int32, (rows, HEAD), 0).astype(F32) + low < jnp.broadcast_to(count, (rows, HEAD))
        for h in range(HEADS_HERE):
            col = h * 3 * HEAD
            query[h, at] = normed(acc[:rows, col : col + HEAD], qk_ref[0, h : h + 1, :]).astype(BF16)
            kv[p, at, h * HEAD : (h + 1) * HEAD] = normed(
                acc[:rows, col + HEAD : col + 2 * HEAD], qk_ref[1, h : h + 1, :]
            ).astype(BF16)
            kv[p, at, WIDE + h * HEAD : WIDE + (h + 1) * HEAD] = jnp.where(
                real, acc[:rows, col + 2 * HEAD : col + 3 * HEAD], 0.0
            ).astype(BF16)

    def attend(c):
        for h in range(HEADS_HERE):
            keys = kv[:, :, h * HEAD : (h + 1) * HEAD].reshape(GROUP * LIVE, HEAD)
            values = kv[:, :, WIDE + h * HEAD : WIDE + (h + 1) * HEAD].reshape(GROUP * LIVE, HEAD)
            scores = (
                lax.dot_general(query[h, c * ROWS : (c + 1) * ROWS], keys, (((1,), (1,)), ((), ())), preferred_element_type=F32) * SCALE
            )
            top = jnp.max(scores, axis=-1, keepdims=True)
            weights = jnp.exp2(scores - top).astype(BF16)
            summed = jnp.dot(
                weights, jnp.concatenate([values, flags[...]], axis=1), preferred_element_type=F32
            )
            heads = (summed[:, :HEAD] / summed[:, HEAD:]).astype(BF16)
            hg[y, x, c * ROWS : (c + 1) * ROWS, h * HEAD : (h + 1) * HEAD] = heads

    def close(c):
        if c == 0:
            load_wo.wait()
        total = jnp.zeros((ROWS, FEAT), F32)
        for b in range(SIDE):
            heads = jnp.concatenate([hg[b, i, c * ROWS : (c + 1) * ROWS] for i in range(SIDE)], axis=1)
            total += jnp.dot(heads, wo[b * SIDE * WIDE : (b + 1) * SIDE * WIDE, :], preferred_element_type=F32)
        mine = xg[y, x, c * ROWS : (c + 1) * ROWS].astype(F32)
        result[c * ROWS : (c + 1) * ROWS, :] = (mine + total).astype(BF16)
        low, high = c * ROWS, (c + 1) * ROWS if c < CHUNKS - 1 else TOK
        known = (c + 1) * ROWS
        placed = jnp.dot(place[low:high, :known], result[:known, :], preferred_element_type=F32)
        outgoing[low:high, :] = (rest[low:high, :].astype(F32) + placed).astype(BF16)
        copy = pltpu.make_async_remote_copy(
            src_ref=outgoing.at[pl.ds(low, high - low)],
            dst_ref=out_ref.at[pl.ds(low, high - low)],
            send_sem=o_send.at[c],
            recv_sem=o_recv.at[c],
            device_id={"section": 1 - s},
            device_id_type=MESH,
        )
        copy.start()
        return copy

    copies = []

    def greet():
        for j in (1, 2, 3):
            count_copy(j - 1, counts.at[p], peers[j - 1]).start()

    def prepare():
        place[...] = jnp.transpose(pick[...]).astype(BF16)
        rest[...] = (
            x_ref[...].astype(F32) - jnp.dot(place[...], compact, preferred_element_type=F32)
        ).astype(BF16)
        for j in (1, 2, 3):
            count_copy(j - 1, counts.at[lax.rem(p + GROUP - j, GROUP)], peers[j - 1]).wait_recv()
        place_of = lax.broadcasted_iota(jnp.int32, (LIVE, HEAD), 0).astype(F32)
        for q in range(GROUP):
            flags[q * LIVE : (q + 1) * LIVE, :] = jnp.where(
                place_of < jnp.broadcast_to(counts[q, 0:1, :], (LIVE, HEAD)), 1.0, 0.0
            ).astype(BF16)

    def gate():
        pl.when(s == 1)(lambda: pl.semaphore_wait(turn, 1))

    def open_gate():
        @pl.when(s == 0)
        def _():
            pl.semaphore_signal(turn, inc=1, device_id={"section": 1 - s}, device_id_type=MESH)

    steps = {
        "a": ga.step, "c": gc.step, "z": line.step, "project": project, "attend": attend,
        "close": lambda c: copies.append(close(c)), "greet": greet, "prepare": prepare,
        "gate": gate, "open": open_gate,
    }
    for name, *at in ORDER:
        steps[name](*at)

    for j in (1, 2, 3):
        count_copy(j - 1, counts.at[p], peers[j - 1]).wait_send()
    ga.finish()
    gc.finish()
    line.finish()
    for copy in copies:
        copy.wait()


def body(acts, halting, norm_gain, qkv_weight, qk_gain, out_weight):
    vmem = pl.BlockSpec(memory_space=pltpu.VMEM)
    anywhere = pl.BlockSpec(memory_space=pl.ANY)
    out = pl.pallas_call(
        kernel,
        out_shape=jax.ShapeDtypeStruct((TOK, FEAT), BF16),
        in_specs=[vmem, vmem, vmem, vmem, anywhere, anywhere],
        out_specs=anywhere,
        scratch_shapes=[
            pltpu.VMEM((16 * FEAT, COLS), BF16),
            pltpu.VMEM((16 * WIDE, FEAT), BF16),
            pltpu.VMEM((SIDE, SIDE, LIVE, FEAT), BF16),
            pltpu.VMEM((ROWS, 16 * FEAT), BF16),
            pltpu.VMEM((ROWS, COLS), F32),
            pltpu.VMEM((GROUP, LIVE, 2 * WIDE), BF16),
            pltpu.VMEM((HEADS_HERE, LIVE, HEAD), BF16),
            pltpu.VMEM((GROUP, 8, 128), F32),
            pltpu.VMEM((GROUP * LIVE, HEAD), BF16),
            pltpu.VMEM((SIDE, SIDE, LIVE, WIDE), BF16),
            pltpu.VMEM((LIVE, TOK), F32),
            pltpu.VMEM((TOK, LIVE), BF16),
            pltpu.VMEM((TOK, FEAT), BF16),
            pltpu.VMEM((LIVE, FEAT), BF16),
            pltpu.VMEM((TOK, FEAT), BF16),
            pltpu.SemaphoreType.DMA((2,)),
            pltpu.SemaphoreType.DMA((len(PIECES_A) * 8,)),
            pltpu.SemaphoreType.DMA((len(PIECES_A) * 8,)),
            pltpu.SemaphoreType.DMA((len(PIECES_C) * 8,)),
            pltpu.SemaphoreType.DMA((len(PIECES_C) * 8,)),
            pltpu.SemaphoreType.DMA((len(PARTS) * 6,)),
            pltpu.SemaphoreType.DMA((len(PARTS) * 6,)),
            pltpu.SemaphoreType.DMA((3,)),
            pltpu.SemaphoreType.DMA((3,)),
            pltpu.SemaphoreType.DMA((CHUNKS,)),
            pltpu.SemaphoreType.DMA((CHUNKS,)),
            pltpu.SemaphoreType.REGULAR,
        ],
        compiler_params=pltpu.CompilerParams(
            collective_id=0, has_side_effects=True, vmem_limit_bytes=56 * 1024 * 1024
        ),
    )(acts[0], halting, norm_gain, qk_gain[0], qkv_weight[0], out_weight[0])
    return out[None]


def solution(mesh):
    return jax.shard_map(
        body,
        mesh=mesh,
        in_specs=(
            P("section", "dp", "mp"),
            P("section", "dp"),
            P("section", None),
            P("section", None, "mp"),
            P("section", None, "mp", None),
            P("section", None, "mp"),
        ),
        out_specs=P("section", "dp", "mp"),
        check_vma=False,
    )
```

time: 98.7 us -> 81.2 us (0.82)
  Pallas kernels: 96.8 us -> 79.2 us
    pallas_call x1, Pallas kernels: 96.8 us -> 79.2 us  [body(): pl.pallas_call(kernel, out_shape=jax.ShapeDtypeStruct((TOK, FEAT), BF16),...]
where the time goes in v2:
time: 81.2 us; the launch traced here: 81 us
  Pallas kernels  79.2 us (98%)
  local copies, waits for them, and re-layouts  1.78 us (2%)
    pallas_call x1, Pallas kernels, body(): pl.pallas_call(kernel, out_shape=jax.ShapeDtypeStruct((TOK, FEAT), BF16),...  79.2 us
    unnamed x1, local copies, waits for them, and re-layouts  1.78 us

profile of v2, /device:TPU:1, one launch (start us, length us, event | category | flops | bytes accessed | tf_op | source)
XLA Modules:
  0.0 81.0 jit_solution(9062155782893283381)
XLA Ops:
  0.0 79.2 %shard_map.64 = bf16[512,384]{1,0:T(8,128)(2,1)} custom-call(bf16[512,384]{1,0:T(8,128)(2,1)} %bitcast.8, s32[1,512]{1,0:T(1,128)} %halt_ref.1, f32[1,6144]{1,0:T(1,128)} %gain_ref.1, f32[2,2,128]{2,1,0:T(2,128)} %bitcast.9, bf16[6144,768]{1,0:T(8,128)(2,1)} %bitcast.5, bf16[4096,384]{1,0:T(8,128)(2,1)} %bitcast.6), custom_call_target="tpu_custom_call" | custom-call | tf_op jit(solution)/shard_map/pallas_call | solution.py:374
  79.2 1.8 %copy.8 = bf16[1,512,384]{2,1,0:T(8,128)(2,1)} copy(bf16[1,512,384]{2,1,0:T(8,128)(2,1)} %bitcast.7) | data formatting | bytes 786432

commit v3 on v2

--- a/solution.py
+++ b/solution.py
@@ -25,23 +25,24 @@
 BF16 = jnp.bfloat16
 
 
-PIECES_A = (
-    (0, 32, 1, 0), (32, 32, 0, 0), (64, 64, 1, 0), (128, 64, 0, 0), (192, 64, 1, 0), (256, 64, 0, 0),
-    (320, 32, 1, 0), (352, 32, 0, 0),
-)
+PIECES_A = ((0, 32, 1, 0), (32, 32, 0, 0), (64, 64, 1, 0), (128, 64, 0, 0), (192, 64, 1, 0), (256, 64, 0, 0), (320, 32, 1, 0), (352, 32, 0, 0))
 PIECES_C = ((0, 64, 1, 1), (64, 64, 0, 1), (128, 64, 1, 1), (192, 64, 0, 1), (256, 64, 1, 1), (320, 64, 0, 1))
 PARTS = ((0, 64), (64, 128), (192, 128), (320, 64))
 
+DIRECT = (3,)
+
 ORDER = (
-    ("gate",), ("a", 0, 0), ("a", 1, 0), ("a", 2, 0), ("a", 3, 0), ("greet",), ("a", 0, 1), ("a", 1, 1), ("a", 4, 0), ("a", 5, 0),
-    ("a", 2, 1), ("a", 3, 1), ("a", 6, 0), ("a", 7, 0), ("a", 4, 1), ("a", 5, 1), ("prepare",), ("a", 0, 2), ("a", 1, 2),
-    ("project", 0), ("z", 0, 0), ("a", 6, 1), ("a", 7, 1), ("open",), ("a", 2, 2), ("a", 3, 2), ("project", 1), ("z", 1, 0),
-    ("z", 0, 1), ("a", 4, 2), ("a", 5, 2), ("project", 2), ("z", 2, 0), ("z", 0, 2), ("z", 1, 1), ("a", 6, 2), ("a", 7, 2),
-    ("project", 3), ("z", 3, 0), ("z", 0, 3), ("z", 1, 2), ("z", 2, 1), ("z", 1, 3), ("z", 3, 1), ("z", 2, 2), ("z", 2, 3), ("z", 3, 2), ("z", 3, 3),
-    ("attend", 0), ("c", 0, 0), ("c", 1, 0), ("attend", 1), ("c", 2, 0), ("c", 3, 0), ("attend", 2), ("c", 4, 0), ("c", 5, 0),
-    ("c", 0, 1), ("c", 1, 1), ("c", 2, 1), ("c", 3, 1), ("c", 4, 1), ("c", 5, 1),
-    ("c", 0, 2), ("c", 1, 2), ("c", 2, 2), ("c", 3, 2), ("c", 4, 2), ("c", 5, 2), ("c", 0, 3), ("c", 1, 3), ("close", 0),
-    ("c", 2, 3), ("c", 3, 3), ("close", 1), ("c", 4, 3), ("c", 5, 3), ("close", 2),
+    ("a", 0, 0), ("a", 0, 1), ("a", 1, 0), ("a", 1, 1), ("gate",), ("a", 2, 0), ("a", 2, 1), ("a", 3, 0), ("a", 3, 1),
+    ("greet",), ("a", 0, 2), ("a", 1, 2), ("a", 4, 0), ("a", 4, 1), ("a", 5, 0), ("a", 5, 1), ("a", 2, 2),
+    ("a", 3, 2), ("a", 6, 0), ("a", 6, 1), ("a", 7, 0), ("a", 7, 1), ("a", 4, 2), ("a", 5, 2), ("prepare",),
+    ("a", 0, 3), ("a", 1, 3), ("project", 0), ("z", 0, 0), ("a", 6, 2), ("a", 7, 2), ("open",), ("a", 2, 3),
+    ("a", 3, 3), ("project", 1), ("z", 1, 0), ("z", 0, 1), ("a", 4, 3), ("a", 5, 3), ("project", 2), ("z", 2, 0),
+    ("z", 1, 1), ("a", 6, 3), ("a", 7, 3), ("project", 3), ("z", 3, 0), ("z", 2, 1), ("z", 0, 2), ("z", 1, 2),
+    ("z", 2, 2), ("z", 3, 2), ("attend", 0), ("c", 0, 0), ("c", 0, 1), ("c", 1, 0), ("c", 1, 1), ("attend", 1),
+    ("c", 2, 0), ("c", 2, 1), ("c", 3, 0), ("c", 3, 1), ("attend", 2), ("c", 4, 0), ("c", 4, 1), ("c", 5, 0),
+    ("c", 5, 1), ("c", 0, 2), ("c", 1, 2), ("c", 2, 2), ("c", 3, 2), ("c", 4, 2), ("c", 5, 2), ("c", 0, 3),
+    ("c", 1, 3), ("c", 2, 3), ("c", 3, 3), ("c", 4, 3), ("c", 5, 3), ("c", 0, 4), ("c", 1, 4), ("close", 0),
+    ("c", 2, 4), ("c", 3, 4), ("close", 1), ("c", 4, 4), ("c", 5, 4), ("close", 2),
 )
 
 
@@ -51,131 +52,140 @@
         self.at = (y, x)
         self.started = []
 
-    def ring(self, axis, by):
-        return lax.rem(self.at[axis] + by + SIDE, SIDE)
-
     def device(self, axis, by):
         y, x = self.at
         if axis == 0:
-            y = self.ring(0, by)
+            y = lax.rem(y + by + SIDE, SIDE)
         else:
-            x = self.ring(1, by)
+            x = lax.rem(x + by + SIDE, SIDE)
         return {"mp": y * SIDE + x}
 
-    def copy(self, ref, n, k, device):
-        at = n * 8 + k
+    def copy(self, n, k, src, dst, device):
+        at = n * 9 + k
+        return pltpu.make_async_remote_copy(
+            src_ref=src,
+            dst_ref=dst,
+            send_sem=self.send.at[at],
+            recv_sem=self.recv.at[at],
+            device_id=device,
+            device_id_type=MESH,
+        )
+
+    def plan(self, n):
+        row, rows, first, way = self.pieces[n]
+        whole = ((0, 1), (1, -1), (2, 2))
+        sends = [[(k, (0, 1), 0, first, d) for k, d in whole]]
+        if way == 0:
+            sends += [[(3 + k, (0, 1), 0, 1 - first, d) for k, d in whole]]
+            sends += [[(6 + k, (1, 3), 0, 1 - first, d) for k, d in whole]]
+            waits = ((), (), (0,), (1, 2))
+        else:
+            sends += [[(3 + k, (0, 1), 0, 1 - first, d) for k, d in whole[:2]]]
+            sends += [[(5 + k, (1, 3), 0, 1 - first, d) for k, d in whole[:2]]]
+            sends += [[(7, (0, 2), -1, 1 - first, 1), (8, (2, 2), 1, 1 - first, -1)]]
+            waits = ((), (), (0,), (1, 2), (3,))
+        return sends, waits
+
+    def ref(self, n, low, count, second):
+        row, rows, first, _ = self.pieces[n]
+        second = second % SIDE
+        if count == 1:
+            y, x = (second, low % SIDE) if first == 1 else (low % SIDE, second)
+            return self.buf.at[y, x, pl.ds(row, rows), :]
+        if first == 1:
+            return self.buf.at[second, pl.ds(low, count), pl.ds(row, rows), :]
+        return self.buf.at[pl.ds(low, count), second, pl.ds(row, rows), :]
+
+    def ends(self, n, at, second, axis, by):
+        low, count = at
+        src = self.ref(n, low, count, second)
+        if axis == self.pieces[n][2]:
+            return src, self.ref(n, low - by, count, second)
+        return src, self.ref(n, low, count, second - by)
+
+    def step(self, n, stage):
+        sends, waits = self.plan(n)
+        for before in waits[stage]:
+            for k, at, second, axis, by in sends[before]:
+                _, dst = self.ends(n, at, second, axis, by)
+                self.copy(n, k, dst, dst, self.device(axis, by)).wait_recv()
+        if stage < len(sends):
+            for k, at, second, axis, by in sends[stage]:
+                copy = self.copy(n, k, *self.ends(n, at, second, axis, by), self.device(axis, by))
+                copy.start()
+                self.started.append(copy)
+
+    def finish(self):
+        for copy in self.started:
+            copy.wait_send()
+
+
+class Line:
+    def __init__(self, kv, send, recv, z):
+        self.kv, self.send, self.recv, self.z = kv, send, recv, z
+        self.p = lax.rem(z, GROUP)
+        self.started = []
+
+    def copy(self, c, d, way, owner, device):
+        at = (c * 3 + d - 1) * 2 + (0 if way > 0 else 1)
+        ref = self.kv.at[owner, pl.ds(*PARTS[c])]
         return pltpu.make_async_remote_copy(
             src_ref=ref,
             dst_ref=ref,
             send_sem=self.send.at[at],
             recv_sem=self.recv.at[at],
-            device_id=device,
+            device_id={"dp": device},
             device_id_type=MESH,
         )
 
-    def plan(self, n):
-        row, rows, first, way = self.pieces[n]
-        second = 1 - first
-        half = rows // 2
-
-        def block(by, low=0, count=rows):
-            a = self.ring(first, by)
-            y, x = (self.at[0], a) if first == 1 else (a, self.at[1])
-            return lambda: self.buf.at[y, x, pl.ds(row + low, count), :]
-
-        def slab(by, low=0, count=SIDE):
-            b = self.ring(second, by)
-            if first == 1:
-                return lambda: self.buf.at[b, pl.ds(low, count), pl.ds(row, rows), :]
-            return lambda: self.buf.at[pl.ds(low, count), b, pl.ds(row, rows), :]
-
-        whole = (1, -1, 2)
-        if way < 2:
-            sends = [[(k, block(0), first, d) for k, d in enumerate(whole)]]
-            arrivals = [[(k, block(-d)) for k, d in enumerate(whole)]]
-        else:
-            sends = [
-                [(0, block(0), first, 1), (1, block(0), first, -1)],
-                [(2, block(-1, 0, half), first, 1), (3, block(1, half, half), first, -1)],
-            ]
-            arrivals = [[(0, block(-1)), (1, block(1))], [(2, block(2, 0, half)), (3, block(2, half, half))]]
-        if way < 1:
-            sends += [[(4 + k, slab(0), second, d) for k, d in enumerate(whole)]]
-            arrivals += [[(4 + k, slab(-d)) for k, d in enumerate(whole)]]
-        else:
-            sends += [
-                [(4, slab(0), second, 1), (5, slab(0), second, -1)],
-                [(6, slab(-1, 0, 2), second, 1), (7, slab(1, 2, 2), second, -1)],
-            ]
-            arrivals += [[(4, slab(-1)), (5, slab(1))], [(6, slab(2, 0, 2)), (7, slab(2, 2, 2))]]
-        return sends, arrivals
-
-    def step(self, n, stage):
-        sends, arrivals = self.plan(n)
-        if stage > 0:
-            for k, ref in arrivals[stage - 1]:
-                self.copy(ref(), n, k, self.device(0, 1)).wait_recv()
-        if stage < len(sends):
-            for k, ref, axis, by in sends[stage]:
-                copy = self.copy(ref(), n, k, self.device(axis, by))
-                copy.start()
-                self.started.append(copy)
+    def reaches(self, d, way):
+        return self.p < GROUP - d if way > 0 else self.p >= d
+
+    def comes(self, d, way):
+        return self.p >= d if way > 0 else self.p < GROUP - d
+
+    def passes(self, way):
+        return self.p == (2 if way > 0 else 1)
+
+    def own(self, c, d, way):
+        return self.copy(c, d, way, self.p, self.z + way * d)
+
+    def passed(self, c, way):
+        return self.copy(c, 3, way, self.p - way * 2, self.z + way)
+
+    def arrival(self, c, d, way):
+        return self.copy(c, d, way, self.p - way * d, self.z - way)
+
+    def far(self, c):
+        return (1, 2, 3) if c in DIRECT else (1, 2)
+
+    def step(self, c, stage):
+        for d in (1, 2, 3):
+            for way in (1, -1):
+                if stage == 0 and d in self.far(c):
+                    pl.when(self.reaches(d, way))(lambda: self.own(c, d, way).start())
+                if stage == 1 and d == 3:
+
+                    @pl.when(self.passes(way))
+                    def _():
+                        self.arrival(c, 2, way).wait_recv()
+                        self.passed(c, way).start()
+
+                if stage == 2:
+                    here = self.comes(d, way)
+                    if d == 2 and c not in DIRECT:
+                        here = jnp.logical_and(here, jnp.logical_not(self.passes(way)))
+                    pl.when(here)(lambda: self.arrival(c, d, way).wait_recv())
+        if stage == 0:
+            self.started.append(c)
 
     def finish(self):
-        for copy in self.started:
-            copy.wait_send()
-
-
-class Line:
-    def __init__(self, kv, send, recv, z):
-        self.kv, self.send, self.recv, self.z = kv, send, recv, z
-        self.p = lax.rem(z, GROUP)
-        self.started = []
-
-    def copy(self, c, j, way):
-        at = (c * 3 + j) * 2 + (0 if way > 0 else 1)
-        ref = self.kv.at[self.p - way * j, pl.ds(*PARTS[c])]
-        return pltpu.make_async_remote_copy(
-            src_ref=ref,
-            dst_ref=ref,
-            send_sem=self.send.at[at],
-            recv_sem=self.recv.at[at],
-            device_id={"dp": self.z + way},
-            device_id_type=MESH,
-        )
-
-    def arriving(self, c, j, way):
-        at = (c * 3 + j) * 2 + (0 if way > 0 else 1)
-        ref = self.kv.at[self.p - way * (j + 1), pl.ds(*PARTS[c])]
-        return pltpu.make_async_remote_copy(
-            src_ref=ref,
-            dst_ref=ref,
-            send_sem=self.send.at[at],
-            recv_sem=self.recv.at[at],
-            device_id={"dp": self.z - way},
-            device_id_type=MESH,
-        )
-
-    def has(self, way, j):
-        return self.p >= j if way > 0 else self.p + j < GROUP
-
-    def sends(self, way, j):
-        more = self.p < GROUP - 1 if way > 0 else self.p > 0
-        return jnp.logical_and(more, self.has(way, j))
-
-    def step(self, c, j):
-        if j < 3:
-            self.started.append((c, j))
-        for way in (1, -1):
-            if j > 0:
-                pl.when(self.has(way, j))(lambda: self.arriving(c, j - 1, way).wait_recv())
-            if j < 3:
-                pl.when(self.sends(way, j))(lambda: self.copy(c, j, way).start())
-
-    def finish(self):
-        for c, j in self.started:
+        for c in self.started:
             for way in (1, -1):
-                pl.when(self.sends(way, j))(lambda: self.copy(c, j, way).wait_send())
+                for d in self.far(c):
+                    pl.when(self.reaches(d, way))(lambda: self.own(c, d, way).wait_send())
+                if c not in DIRECT:
+                    pl.when(self.passes(way))(lambda: self.passed(c, way).wait_send())
 
 
 def normed(values, gain):
@@ -230,10 +240,13 @@
     first = jnp.where(chosen, 1.0, 0.0)
     pick[...] = jnp.where(row < jnp.broadcast_to(count, (LIVE, TOK)), first, 0.0)
     compact = jnp.dot(first.astype(BF16), x_ref[...], preferred_element_type=F32).astype(BF16)
-    xg[y, x] = compact
+    xg[0, 0] = compact
     counts[p] = jnp.broadcast_to(count, (8, 128))
 
     pl.semaphore_wait(barrier, 10)
+
+    def from_here(b):
+        return lax.rem(b // SIDE - y + SIDE, SIDE), lax.rem(b % SIDE - x + SIDE, SIDE)
 
     ga = Gather(xg, PIECES_A, a_send, a_recv, x, y)
     gc = Gather(hg, PIECES_C, c_send, c_recv, x, y)
@@ -255,16 +268,16 @@
             at = slice(at, at + 64)
             total = jnp.zeros((64, 1), F32)
             for b in range(16):
-                total += jnp.sum(xg[b // SIDE, b % SIDE, at].astype(F32), axis=-1, keepdims=True)
+                total += jnp.sum(xg[*from_here(b), at].astype(F32), axis=-1, keepdims=True)
             mean = total * (1.0 / (16 * FEAT))
             square = jnp.zeros((64, 1), F32)
             for b in range(16):
-                centred = xg[b // SIDE, b % SIDE, at].astype(F32) - mean
+                centred = xg[*from_here(b), at].astype(F32) - mean
                 square += jnp.sum(centred * centred, axis=-1, keepdims=True)
             scale = lax.rsqrt(square * (1.0 / (16 * FEAT)) + 1e-06)
             for b in range(16):
                 lanes = slice(b * FEAT, (b + 1) * FEAT)
-                centred = xg[b // SIDE, b % SIDE, at].astype(F32) - mean
+                centred = xg[*from_here(b), at].astype(F32) - mean
                 xn[at.start - low : at.stop - low, lanes] = (centred * scale * gain_ref[:, lanes]).astype(BF16)
         if c == 0:
             load_w.wait()
@@ -298,16 +311,18 @@
                 weights, jnp.concatenate([values, flags[...]], axis=1), preferred_element_type=F32
             )
             heads = (summed[:, :HEAD] / summed[:, HEAD:]).astype(BF16)
-            hg[y, x, c * ROWS : (c + 1) * ROWS, h * HEAD : (h + 1) * HEAD] = heads
+            hg[0, 0, c * ROWS : (c + 1) * ROWS, h * HEAD : (h + 1) * HEAD] = heads
 
     def close(c):
         if c == 0:
             load_wo.wait()
         total = jnp.zeros((ROWS, FEAT), F32)
         for b in range(SIDE):
-            heads = jnp.concatenate([hg[b, i, c * ROWS : (c + 1) * ROWS] for i in range(SIDE)], axis=1)
+            heads = jnp.concatenate(
+                [hg[*from_here(b * SIDE + i), c * ROWS : (c + 1) * ROWS] for i in range(SIDE)], axis=1
+            )
             total += jnp.dot(heads, wo[b * SIDE * WIDE : (b + 1) * SIDE * WIDE, :], preferred_element_type=F32)
-        mine = xg[y, x, c * ROWS : (c + 1) * ROWS].astype(F32)
+        mine = xg[0, 0, c * ROWS : (c + 1) * ROWS].astype(F32)
         result[c * ROWS : (c + 1) * ROWS, :] = (mine + total).astype(BF16)
         low, high = c * ROWS, (c + 1) * ROWS if c < CHUNKS - 1 else TOK
         known = (c + 1) * ROWS
@@ -393,10 +408,10 @@
             pltpu.VMEM((LIVE, FEAT), BF16),
             pltpu.VMEM((TOK, FEAT), BF16),
             pltpu.SemaphoreType.DMA((2,)),
-            pltpu.SemaphoreType.DMA((len(PIECES_A) * 8,)),
-            pltpu.SemaphoreType.DMA((len(PIECES_A) * 8,)),
-            pltpu.SemaphoreType.DMA((len(PIECES_C) * 8,)),
-            pltpu.SemaphoreType.DMA((len(PIECES_C) * 8,)),
+            pltpu.SemaphoreType.DMA((len(PIECES_A) * 9,)),
+            pltpu.SemaphoreType.DMA((len(PIECES_A) * 9,)),
+            pltpu.SemaphoreType.DMA((len(PIECES_C) * 9,)),
+            pltpu.SemaphoreType.DMA((len(PIECES_C) * 9,)),
             pltpu.SemaphoreType.DMA((len(PARTS) * 6,)),
             pltpu.SemaphoreType.DMA((len(PARTS) * 6,)),
             pltpu.SemaphoreType.DMA((3,)),

time: 81.2 us -> 77.3 us (0.952)
  Pallas kernels: 79.2 us -> 75.4 us
    pallas_call x1, Pallas kernels: 79.2 us -> 75.4 us  [body(): pl.pallas_call(kernel, out_shape=jax.ShapeDtypeStruct((TOK, FEAT), BF16),...]
where the time goes in v3:
time: 77.3 us; the launch traced here: 77.2 us
  Pallas kernels  75.4 us (98%)
  local copies, waits for them, and re-layouts  1.78 us (2%)
    pallas_call x1, Pallas kernels, body(): pl.pallas_call(kernel, out_shape=jax.ShapeDtypeStruct((TOK, FEAT), BF16),...  75.4 us
    unnamed x1, local copies, waits for them, and re-layouts  1.78 us

profile of v3, /device:TPU:1, one launch (start us, length us, event | category | flops | bytes accessed | tf_op | source)
XLA Modules:
  0.0 77.2 jit_solution(5030482458227288098)
XLA Ops:
  0.0 75.4 %shard_map.64 = bf16[512,384]{1,0:T(8,128)(2,1)} custom-call(bf16[512,384]{1,0:T(8,128)(2,1)} %bitcast.8, s32[1,512]{1,0:T(1,128)} %halt_ref.1, f32[1,6144]{1,0:T(1,128)} %gain_ref.1, f32[2,2,128]{2,1,0:T(2,128)} %bitcast.9, bf16[6144,768]{1,0:T(8,128)(2,1)} %bitcast.5, bf16[4096,384]{1,0:T(8,128)(2,1)} %bitcast.6), custom_call_target="tpu_custom_call" | custom-call | tf_op jit(solution)/shard_map/pallas_call | solution.py:389
  75.4 1.8 %copy.8 = bf16[1,512,384]{2,1,0:T(8,128)(2,1)} copy(bf16[1,512,384]{2,1,0:T(8,128)(2,1)} %bitcast.7) | data formatting | bytes 786432

commit v4 on v3

--- a/solution.py
+++ b/solution.py
@@ -35,9 +35,9 @@
     ("a", 0, 0), ("a", 0, 1), ("a", 1, 0), ("a", 1, 1), ("gate",), ("a", 2, 0), ("a", 2, 1), ("a", 3, 0), ("a", 3, 1),
     ("greet",), ("a", 0, 2), ("a", 1, 2), ("a", 4, 0), ("a", 4, 1), ("a", 5, 0), ("a", 5, 1), ("a", 2, 2),
     ("a", 3, 2), ("a", 6, 0), ("a", 6, 1), ("a", 7, 0), ("a", 7, 1), ("a", 4, 2), ("a", 5, 2), ("prepare",),
-    ("a", 0, 3), ("a", 1, 3), ("project", 0), ("z", 0, 0), ("a", 6, 2), ("a", 7, 2), ("open",), ("a", 2, 3),
-    ("a", 3, 3), ("project", 1), ("z", 1, 0), ("z", 0, 1), ("a", 4, 3), ("a", 5, 3), ("project", 2), ("z", 2, 0),
-    ("z", 1, 1), ("a", 6, 3), ("a", 7, 3), ("project", 3), ("z", 3, 0), ("z", 2, 1), ("z", 0, 2), ("z", 1, 2),
+    ("a", 0, 3), ("a", 1, 3), ("project", 0), ("z", 0, 0), ("ask", 0), ("a", 6, 2), ("a", 7, 2), ("open",), ("a", 2, 3),
+    ("a", 3, 3), ("project", 1), ("z", 1, 0), ("ask", 1), ("z", 0, 1), ("a", 4, 3), ("a", 5, 3), ("project", 2), ("z", 2, 0), ("ask", 2),
+    ("z", 1, 1), ("a", 6, 3), ("a", 7, 3), ("project", 3), ("z", 3, 0), ("ask", 3), ("z", 2, 1), ("z", 0, 2), ("z", 1, 2),
     ("z", 2, 2), ("z", 3, 2), ("attend", 0), ("c", 0, 0), ("c", 0, 1), ("c", 1, 0), ("c", 1, 1), ("attend", 1),
     ("c", 2, 0), ("c", 2, 1), ("c", 3, 0), ("c", 3, 1), ("attend", 2), ("c", 4, 0), ("c", 4, 1), ("c", 5, 0),
     ("c", 5, 1), ("c", 0, 2), ("c", 1, 2), ("c", 2, 2), ("c", 3, 2), ("c", 4, 2), ("c", 5, 2), ("c", 0, 3),
@@ -197,7 +197,7 @@
 
 def kernel(
     x_ref, halt_ref, gain_ref, qk_ref, w_hbm, wo_hbm, out_ref,
-    w, wo, xg, xn, acc, kv, query, counts, flags, hg, pick, place, rest, result, outgoing,
+    w, wo, xg, xn, kv, query, counts, flags, hg, pick, place, rest, result, outgoing,
     w_sem, a_send, a_recv, c_send, c_recv, z_send, z_recv, n_send, n_recv, o_send, o_recv, turn,
 ):
     z = lax.axis_index("dp")
@@ -281,21 +281,27 @@
                 xn[at.start - low : at.stop - low, lanes] = (centred * scale * gain_ref[:, lanes]).astype(BF16)
         if c == 0:
             load_w.wait()
-        total = jnp.zeros((rows, COLS), F32)
+        real = lax.broadcasted_iota(jnp.int32, (rows, HEAD), 0).astype(F32) + low < jnp.broadcast_to(count, (rows, HEAD))
+        at = slice(low, low + rows)
+        for h in range(HEADS_HERE):
+            col = h * 3 * HEAD + HEAD
+            total = jnp.zeros((rows, 2 * HEAD), F32)
+            for b in range(8):
+                depth = slice(b * 2 * FEAT, (b + 1) * 2 * FEAT)
+                total += jnp.dot(xn[:rows, depth], w[depth, col : col + 2 * HEAD], preferred_element_type=F32)
+            kv[p, at, h * HEAD : (h + 1) * HEAD] = normed(total[:, :HEAD], qk_ref[1, h : h + 1, :]).astype(BF16)
+            kv[p, at, WIDE + h * HEAD : WIDE + (h + 1) * HEAD] = jnp.where(real, total[:, HEAD:], 0.0).astype(BF16)
+
+    def ask(c):
+        low, rows = PARTS[c]
+        total = jnp.zeros((rows, WIDE), F32)
         for b in range(8):
             depth = slice(b * 2 * FEAT, (b + 1) * 2 * FEAT)
-            total += jnp.dot(xn[:rows, depth], w[depth, :], preferred_element_type=F32)
-        acc[:rows] = total
-        at = slice(low, low + rows)
-        real = lax.broadcasted_iota(jnp.int32, (rows, HEAD), 0).astype(F32) + low < jnp.broadcast_to(count, (rows, HEAD))
+            columns = jnp.concatenate([w[depth, :HEAD], w[depth, 3 * HEAD : 4 * HEAD]], axis=1)
+            total += jnp.dot(xn[:rows, depth], columns, preferred_element_type=F32)
         for h in range(HEADS_HERE):
-            col = h * 3 * HEAD
-            query[h, at] = normed(acc[:rows, col : col + HEAD], qk_ref[0, h : h + 1, :]).astype(BF16)
-            kv[p, at, h * HEAD : (h + 1) * HEAD] = normed(
-                acc[:rows, col + HEAD : col + 2 * HEAD], qk_ref[1, h : h + 1, :]
-            ).astype(BF16)
-            kv[p, at, WIDE + h * HEAD : WIDE + (h + 1) * HEAD] = jnp.where(
-                real, acc[:rows, col + 2 * HEAD : col + 3 * HEAD], 0.0
+            query[h, low : low + rows] = normed(
+                total[:, h * HEAD : (h + 1) * HEAD], qk_ref[0, h : h + 1, :]
             ).astype(BF16)
 
     def attend(c):
@@ -367,7 +373,7 @@
             pl.semaphore_signal(turn, inc=1, device_id={"section": 1 - s}, device_id_type=MESH)
 
     steps = {
-        "a": ga.step, "c": gc.step, "z": line.step, "project": project, "attend": attend,
+        "a": ga.step, "c": gc.step, "z": line.step, "project": project, "ask": ask, "attend": attend,
         "close": lambda c: copies.append(close(c)), "greet": greet, "prepare": prepare,
         "gate": gate, "open": open_gate,
     }
@@ -396,7 +402,6 @@
             pltpu.VMEM((16 * WIDE, FEAT), BF16),
             pltpu.VMEM((SIDE, SIDE, LIVE, FEAT), BF16),
             pltpu.VMEM((ROWS, 16 * FEAT), BF16),
-            pltpu.VMEM((ROWS, COLS), F32),
             pltpu.VMEM((GROUP, LIVE, 2 * WIDE), BF16),
             pltpu.VMEM((HEADS_HERE, LIVE, HEAD), BF16),
             pltpu.VMEM((GROUP, 8, 128), F32),

time: 77.3 us -> 74.7 us (0.966)
  Pallas kernels: 75.4 us -> 72.8 us
    pallas_call x1, Pallas kernels: 75.4 us -> 72.8 us  [body(): pl.pallas_call(kernel, out_shape=jax.ShapeDtypeStruct((TOK, FEAT), BF16),...]
where the time goes in v4:
time: 74.7 us; the launch traced here: 74.6 us
  Pallas kernels  72.8 us (97%)
  local copies, waits for them, and re-layouts  1.78 us (2%)
    pallas_call x1, Pallas kernels, body(): pl.pallas_call(kernel, out_shape=jax.ShapeDtypeStruct((TOK, FEAT), BF16),...  72.8 us
    unnamed x1, local copies, waits for them, and re-layouts  1.78 us

profile of v4, /device:TPU:1, one launch (start us, length us, event | category | flops | bytes accessed | tf_op | source)
XLA Modules:
  0.0 74.6 jit_solution(8739891352235433510)
XLA Ops:
  0.0 72.8 %shard_map.64 = bf16[512,384]{1,0:T(8,128)(2,1)} custom-call(bf16[512,384]{1,0:T(8,128)(2,1)} %bitcast.8, s32[1,512]{1,0:T(1,128)} %halt_ref.1, f32[1,6144]{1,0:T(1,128)} %gain_ref.1, f32[2,2,128]{2,1,0:T(2,128)} %bitcast.9, bf16[6144,768]{1,0:T(8,128)(2,1)} %bitcast.5, bf16[4096,384]{1,0:T(8,128)(2,1)} %bitcast.6), custom_call_target="tpu_custom_call" | custom-call | tf_op jit(solution)/shard_map/pallas_call | solution.py:395
  72.8 1.8 %copy.8 = bf16[1,512,384]{2,1,0:T(8,128)(2,1)} copy(bf16[1,512,384]{2,1,0:T(8,128)(2,1)} %bitcast.7) | data formatting | bytes 786432

commit v5 on v4

--- a/solution.py
+++ b/solution.py
@@ -36,8 +36,8 @@
     ("greet",), ("a", 0, 2), ("a", 1, 2), ("a", 4, 0), ("a", 4, 1), ("a", 5, 0), ("a", 5, 1), ("a", 2, 2),
     ("a", 3, 2), ("a", 6, 0), ("a", 6, 1), ("a", 7, 0), ("a", 7, 1), ("a", 4, 2), ("a", 5, 2), ("prepare",),
     ("a", 0, 3), ("a", 1, 3), ("project", 0), ("z", 0, 0), ("ask", 0), ("a", 6, 2), ("a", 7, 2), ("open",), ("a", 2, 3),
-    ("a", 3, 3), ("project", 1), ("z", 1, 0), ("ask", 1), ("z", 0, 1), ("a", 4, 3), ("a", 5, 3), ("project", 2), ("z", 2, 0), ("ask", 2),
-    ("z", 1, 1), ("a", 6, 3), ("a", 7, 3), ("project", 3), ("z", 3, 0), ("ask", 3), ("z", 2, 1), ("z", 0, 2), ("z", 1, 2),
+    ("a", 3, 3), ("project", 1), ("z", 1, 0), ("z", 0, 1), ("ask", 1), ("a", 4, 3), ("a", 5, 3), ("project", 2), ("z", 2, 0), ("z", 1, 1),
+    ("ask", 2), ("a", 6, 3), ("a", 7, 3), ("project", 3), ("z", 3, 0), ("z", 2, 1), ("ask", 3), ("z", 0, 2), ("z", 1, 2),
     ("z", 2, 2), ("z", 3, 2), ("attend", 0), ("c", 0, 0), ("c", 0, 1), ("c", 1, 0), ("c", 1, 1), ("attend", 1),
     ("c", 2, 0), ("c", 2, 1), ("c", 3, 0), ("c", 3, 1), ("attend", 2), ("c", 4, 0), ("c", 4, 1), ("c", 5, 0),
     ("c", 5, 1), ("c", 0, 2), ("c", 1, 2), ("c", 2, 2), ("c", 3, 2), ("c", 4, 2), ("c", 5, 2), ("c", 0, 3),

time: 74.7 us -> 74.9 us (level)
  no operation moved by 1% of the time
where the time goes in v5:
time: 74.9 us; the launch traced here: 74.7 us
  Pallas kernels  73 us (97%)
  local copies, waits for them, and re-layouts  1.78 us (2%)
    pallas_call x1, Pallas kernels, body(): pl.pallas_call(kernel, out_shape=jax.ShapeDtypeStruct((TOK, FEAT), BF16),...  73 us
    unnamed x1, local copies, waits for them, and re-layouts  1.78 us

profile of v5, /device:TPU:1, one launch (start us, length us, event | category | flops | bytes accessed | tf_op | source)
XLA Modules:
  0.0 74.7 jit_solution(8244658463443553022)
XLA Ops:
  0.0 73.0 %shard_map.64 = bf16[512,384]{1,0:T(8,128)(2,1)} custom-call(bf16[512,384]{1,0:T(8,128)(2,1)} %bitcast.8, s32[1,512]{1,0:T(1,128)} %halt_ref.1, f32[1,6144]{1,0:T(1,128)} %gain_ref.1, f32[2,2,128]{2,1,0:T(2,128)} %bitcast.9, bf16[6144,768]{1,0:T(8,128)(2,1)} %bitcast.5, bf16[4096,384]{1,0:T(8,128)(2,1)} %bitcast.6), custom_call_target="tpu_custom_call" | custom-call | tf_op jit(solution)/shard_map/pallas_call | solution.py:395
  73.0 1.8 %copy.8 = bf16[1,512,384]{2,1,0:T(8,128)(2,1)} copy(bf16[1,512,384]{2,1,0:T(8,128)(2,1)} %bitcast.7) | data formatting | bytes 786432

commit v6 on v4

--- a/solution.py
+++ b/solution.py
@@ -26,7 +26,7 @@
 
 
 PIECES_A = ((0, 32, 1, 0), (32, 32, 0, 0), (64, 64, 1, 0), (128, 64, 0, 0), (192, 64, 1, 0), (256, 64, 0, 0), (320, 32, 1, 0), (352, 32, 0, 0))
-PIECES_C = ((0, 64, 1, 1), (64, 64, 0, 1), (128, 64, 1, 1), (192, 64, 0, 1), (256, 64, 1, 1), (320, 64, 0, 1))
+PIECES_C = ((0, 64, 1, 1), (64, 64, 0, 1), (128, 64, 1, 1), (192, 64, 0, 1), (256, 64, 1, 0), (320, 64, 0, 0))
 PARTS = ((0, 64), (64, 128), (192, 128), (320, 64))
 
 DIRECT = (3,)
@@ -41,8 +41,8 @@
     ("z", 2, 2), ("z", 3, 2), ("attend", 0), ("c", 0, 0), ("c", 0, 1), ("c", 1, 0), ("c", 1, 1), ("attend", 1),
     ("c", 2, 0), ("c", 2, 1), ("c", 3, 0), ("c", 3, 1), ("attend", 2), ("c", 4, 0), ("c", 4, 1), ("c", 5, 0),
     ("c", 5, 1), ("c", 0, 2), ("c", 1, 2), ("c", 2, 2), ("c", 3, 2), ("c", 4, 2), ("c", 5, 2), ("c", 0, 3),
-    ("c", 1, 3), ("c", 2, 3), ("c", 3, 3), ("c", 4, 3), ("c", 5, 3), ("c", 0, 4), ("c", 1, 4), ("close", 0),
-    ("c", 2, 4), ("c", 3, 4), ("close", 1), ("c", 4, 4), ("c", 5, 4), ("close", 2),
+    ("c", 1, 3), ("c", 2, 3), ("c", 3, 3), ("c", 0, 4), ("c", 1, 4), ("close", 0),
+    ("c", 2, 4), ("c", 3, 4), ("close", 1), ("c", 4, 3), ("c", 5, 3), ("close", 2),
 )
 
 

time: 74.7 us -> 75.3 us (level)
  no operation moved by 1% of the time
where the time goes in v6:
time: 75.3 us; the launch traced here: 75.2 us
  Pallas kernels  73.4 us (97%)
  local copies, waits for them, and re-layouts  1.78 us (2%)
    pallas_call x1, Pallas kernels, body(): pl.pallas_call(kernel, out_shape=jax.ShapeDtypeStruct((TOK, FEAT), BF16),...  73.4 us
    unnamed x1, local copies, waits for them, and re-layouts  1.78 us

profile of v6, /device:TPU:1, one launch (start us, length us, event | category | flops | bytes accessed | tf_op | source)
XLA Modules:
  0.0 75.2 jit_solution(10795756707372356070)
XLA Ops:
  0.0 73.4 %shard_map.64 = bf16[512,384]{1,0:T(8,128)(2,1)} custom-call(bf16[512,384]{1,0:T(8,128)(2,1)} %bitcast.8, s32[1,512]{1,0:T(1,128)} %halt_ref.1, f32[1,6144]{1,0:T(1,128)} %gain_ref.1, f32[2,2,128]{2,1,0:T(2,128)} %bitcast.9, bf16[6144,768]{1,0:T(8,128)(2,1)} %bitcast.5, bf16[4096,384]{1,0:T(8,128)(2,1)} %bitcast.6), custom_call_target="tpu_custom_call" | custom-call | tf_op jit(solution)/shard_map/pallas_call | solution.py:395
  73.4 1.8 %copy.8 = bf16[1,512,384]{2,1,0:T(8,128)(2,1)} copy(bf16[1,512,384]{2,1,0:T(8,128)(2,1)} %bitcast.7) | data formatting | bytes 786432
